TPU v7x, 256 devices: a whole 4x4x8 slice. The times are simulated.
256 devices in a mesh: dom: 128 (over x, y, z_hi, core), band: 2 (over z_lo).
Axes of the slice: x: 4, y: 4, z: 8 (z_hi: 4, z_lo: 2; z = z_hi * 2 + z_lo), core: 2. Of those that a mesh axis runs over, the one named last changes fastest.
Arguments:
- orbitals: float32 [128, 2, 12, 32, 1024], P('dom', 'band'), may hold values from -500 to 500
- potential: float32 [128, 12, 32, 32], P('dom'), may hold values from -40 to 0
Outputs:
- orbitals_out: float32 [128, 2, 12, 32, 1024], P('dom', 'band')
- projected: float32 [64, 64], replicated
All inputs are finite; a program needn't handle non-finite values.
Results may differ from a plain program's by a relative error of at most 0.00016.
Values sent between devices are 32-bit elements; how exact they have to be, the bound alone decides.
A program may use at most 64 MiB of HBM per device.

v0:
```python
import jax
import jax.numpy as jnp
from jax import lax
from jax.sharding import PartitionSpec as P

OB = 32
PY = 4
PZ = 4


COEFFS = (
    -5369.0 / 1800.0,
    12.0 / 7.0,
    -15.0 / 56.0,
    10.0 / 189.0,
    -1.0 / 112.0,
    2.0 / 1925.0,
    -1.0 / 16632.0,
)
SPACING = 0.32
CENTER = 71.0
HALFWIDTH = 69.0


def passed_along(x, axis, by):
    length = lax.axis_size(axis)
    pairs = [(i, i + by) for i in range(length) if 0 <= i + by < length]
    return lax.ppermute(x, axis, pairs)


def extend(field, dim, depth, stride, low_valid, high_valid):
    extent = field.shape[dim]
    upper_rim = lax.slice_in_dim(field, extent - depth, extent, axis=dim)
    lower_rim = lax.slice_in_dim(field, 0, depth, axis=dim)
    below = passed_along(upper_rim, "dom", stride) * low_valid
    above = passed_along(lower_rim, "dom", -stride) * high_valid
    return jnp.concatenate([below, field, above], axis=dim)


def scaled_operator(field, pot_tile, valid):
    cx, cy, zo = field.shape
    ext_x = extend(field, 0, 6, PY * PZ, 1.0, 1.0)
    ext_y = extend(field, 1, 6, PZ, valid[0], valid[1])
    ext_z = extend(field, 2, 6 * OB, 1, valid[2], valid[3])
    lap = 3.0 * COEFFS[0] * field
    for shift in range(1, 7):
        terms = ext_x[6 + shift : 6 + shift + cx] + ext_x[6 - shift : 6 - shift + cx]
        terms = terms + ext_y[:, 6 + shift : 6 + shift + cy] + ext_y[:, 6 - shift : 6 - shift + cy]
        terms = (
            terms
            + ext_z[:, :, (6 + shift) * OB : (6 + shift) * OB + zo]
            + ext_z[:, :, (6 - shift) * OB : (6 - shift) * OB + zo]
        )
        lap = lap + COEFFS[shift] * terms
    potential_term = (pot_tile[:, :, :, None] * field.reshape(cx, cy, zo // OB, OB)).reshape(
        cx, cy, zo
    )
    return (-0.5 / SPACING**2 * lap + potential_term - CENTER * field) / HALFWIDTH


def local(orbitals, potential):
    highest = lax.Precision.HIGHEST
    field = orbitals[0, 0]
    cx, cy, zo = field.shape
    pot_tile = potential[0]
    tile = lax.axis_index("dom")
    tile_z = tile % PZ
    tile_y = tile // PZ % PY
    valid = (
        (tile_y > 0).astype(jnp.float32),
        (tile_y < PY - 1).astype(jnp.float32),
        (tile_z > 0).astype(jnp.float32),
        (tile_z < PZ - 1).astype(jnp.float32),
    )
    first = scaled_operator(field, pot_tile, valid)
    filtered = 2.0 * scaled_operator(first, pot_tile, valid) - field
    image = scaled_operator(filtered, pot_tile, valid)
    cells = cx * cy * (zo // OB)
    filt_mat = filtered.reshape(cells, OB)
    image_mat = image.reshape(cells, OB)
    stacked = filt_mat[None]
    band_index = lax.axis_index("band")
    band_count = lax.axis_size("band")
    total_orb = OB * band_count
    cells_all = cells * lax.axis_size("dom")
    every_block = lax.all_gather(stacked, "band", axis=0, tiled=True)
    count = every_block.shape[0]
    over_rows = jnp.einsum("cp,kcq->pkq", filt_mat, every_block, precision=highest).reshape(
        OB, count * OB
    )
    ham_rows = jnp.einsum("cp,kcq->pkq", image_mat, every_block, precision=highest).reshape(
        OB, count * OB
    )
    over_sum, hamt_sum = lax.psum((over_rows, ham_rows), "dom")
    correlation, hamt = (
        lax.all_gather(over_sum, "band", axis=0, tiled=True),
        lax.all_gather(hamt_sum, "band", axis=0, tiled=True),
    )
    correlation = correlation / cells_all
    hamiltonian = hamt.T / cells_all
    lower = jnp.linalg.cholesky(correlation)
    inverse = jax.scipy.linalg.solve_triangular(
        lower, jnp.eye(total_orb, dtype=jnp.float32), lower=True
    )
    projected = jnp.dot(
        jnp.dot(inverse, hamiltonian, precision=highest), inverse.T, precision=highest
    )
    coeffs = lax.dynamic_slice_in_dim(inverse, band_index * OB, OB, 0).T
    count = every_block.shape[0]
    part_coeffs = coeffs.reshape(count, OB, OB)
    rotated = jnp.einsum("kcq,kqp->cp", every_block, part_coeffs, precision=highest)
    return (rotated.reshape(1, 1, cx, cy, zo), projected)


def solution(mesh):
    return jax.shard_map(
        local,
        mesh=mesh,
        in_specs=(P("dom", "band", None, None, None), P("dom", None, None, None)),
        out_specs=(P("dom", "band", None, None, None), P()),
        check_vma=False,
    )
```

profile of v0, /device:TPU:33, one launch (start us, length us, event | category | flops | bytes accessed | tf_op | source)
XLA Modules:
  0.0 1041.9 jit_solution(4966345487436236509)
XLA Ops:
  7.2 2.3 fusion.245
  9.5 5.4 collective-permute-start.5
  14.9 1.9 collective-permute-start.4
  16.9 0.9 fusion.244
  17.8 6.9 collective-permute-start.3
  24.7 1.4 collective-permute-start.2
  26.1 1.3 slice_bitcast_fusion.1
  27.4 7.7 collective-permute-start.1
  35.1 3.8 mul.194
  38.9 5.0 mul.195
  44.0 0.8 copy-done.8
  44.8 1.3 collective-permute-start
  46.1 1.0 broadcast_multiply_fusion.3
  47.1 1.8 broadcast_multiply_fusion.6
  48.9 1.8 broadcast_multiply_fusion.9
  50.7 14.4 %collective-permute-done.2 = f32[12,6,1024]{2,1,0:T(8,128)} collective-permute-done((f32[12,6,1024]{2,1,0:T(8,128)}, f32[12,6,1024]{2,1,0:T(8,128)}, u32[]{:S(2)}, u32[]{:S(2)}) %collective-permute-start.2) | collective-permute-done | bytes 294944 | tf_op jit(solution)/shard_map/ppermute | solution.py:28
  65.1 1.8 broadcast_multiply_fusion.12
  66.8 8.6 collective-permute-done.1
  75.5 17.5 %broadcast_multiply_fusion = (f32[12,32,1024]{2,1,0:T(8,128)S(1)}, f32[12,32,1024]{2,1,0:T(8,128)}) fusion(f32[12,32,1024]{2,1,0:T(8,128)S(1)} %bitcast.39, f32[12,32,1024]{2,1,0:T(8,128)S(1)} %mul.195, f32[12,32,192]{2,1,0:T(8,128)S(1)} %broadcast_multiply_fusion.3, f32[12,32,192]{2,1,0:T(8,128)} %broadcast_multiply_fusion.6, ...), kind=kLoop, calls=%fused_computation.427 | loop fusion | flops 33423360 | bytes 9043968 | tf_op jit(solution)/shard_map/div | solution.py:58
  93.2 4.0 collective-permute-start.11
  97.4 2.3 collective-permute-start.10
  99.7 1.3 collective-permute-start.9
  101.1 1.3 collective-permute-start.8
  102.4 13.8 %collective-permute-start.7 = (f32[6,32,1024]{2,1,0:T(8,128)S(1)}, f32[6,32,1024]{2,1,0:T(8,128)S(1)}, u32[]{:S(2)}, u32[]{:S(2)}) collective-permute-start(f32[6,32,1024]{2,1,0:T(8,128)S(1)} %get-tuple-element.13), channel_id=1, source_target_pairs={{0,32},{2,34},{4,36},{6,38},{8,40},{10,42},{12,44},{14,46},{16,48}... | collective-permute-start | bytes 2359304 | tf_op jit(solution)/shard_map/ppermute | solution.py:28
  116.2 1.5 collective-permute-start.6
  117.7 0.8 broadcast_multiply_fusion.5
  118.5 0.8 broadcast_multiply_fusion.8
  119.3 22.6 %collective-permute-done.8 = f32[12,6,1024]{2,1,0:T(8,128)S(1)} collective-permute-done((f32[12,6,1024]{2,1,0:T(8,128)S(1)}, f32[12,6,1024]{2,1,0:T(8,128)S(1)}, u32[]{:S(2)}, u32[]{:S(2)}) %collective-permute-start.8) | collective-permute-done | bytes 294944 | tf_op jit(solution)/shard_map/ppermute | solution.py:28
  141.9 0.8 broadcast_multiply_fusion.11
  142.7 13.8 %collective-permute-done.7 = f32[6,32,1024]{2,1,0:T(8,128)S(1)} collective-permute-done((f32[6,32,1024]{2,1,0:T(8,128)S(1)}, f32[6,32,1024]{2,1,0:T(8,128)S(1)}, u32[]{:S(2)}, u32[]{:S(2)}) %collective-permute-start.7) | collective-permute-done | bytes 786464 | tf_op jit(solution)/shard_map/ppermute | solution.py:28
  156.5 0.9 copy-done.6
  157.4 0.9 copy-done.7
  158.4 17.4 %fusion.64 = f32[12,32,1024]{2,1,0:T(8,128)S(1)} fusion(f32[12,32,1024]{2,1,0:T(8,128)S(1)} %get-tuple-element.4, f32[12,32,192]{2,1,0:T(8,128)S(1)} %broadcast_multiply_fusion.2, f32[12,32,192]{2,1,0:T(8,128)} %broadcast_multiply_fusion.5, f32[12,6,1024]{2,1,0:T(8,128)} %broadcast_multiply_fusion.8, f32[12,6,1024]{2,1,0:T(8,128)} %broadcast_multiply_fusion.11, ...), kind=kLoop, calls=%fused_computation.245 | loop fusion | flops 33816576 | bytes 10616832 | tf_op jit(solution)/shard_map/sub | solution.py:76
  175.8 4.1 broadcast_in_dim_reshape.3
  179.9 1.0 fusion.240
  180.9 5.5 copy.12
  186.5 7.2 collective-permute-start.17
  193.8 1.9 collective-permute-start.16
  195.8 1.0 fusion.239
  196.7 4.1 reshape.42
  200.8 1.3 collective-permute-start.15
  202.1 1.3 collective-permute-start.14
  203.4 17.5 %collective-permute-start.13 = (f32[6,32,1024]{2,1,0:T(8,128)S(1)}, f32[6,32,1024]{2,1,0:T(8,128)S(1)}, u32[]{:S(2)}, u32[]{:S(2)}) collective-permute-start(f32[6,32,1024]{2,1,0:T(8,128)S(1)} %get-tuple-element.7), channel_id=1, source_target_pairs={{0,32},{2,34},{4,36},{6,38},{8,40},{10,42},{12,44},{14,46},{16,48}... | collective-permute-start | bytes 2359304 | tf_op jit(solution)/shard_map/ppermute | solution.py:28
  220.9 1.4 collective-permute-start.12
  222.4 1.0 broadcast_multiply_fusion.1
  223.4 1.0 broadcast_multiply_fusion.4
  224.5 8.1 collective-permute-done.14
  232.6 26.0 %collective-permute-done.13 = f32[6,32,1024]{2,1,0:T(8,128)S(1)} collective-permute-done((f32[6,32,1024]{2,1,0:T(8,128)S(1)}, f32[6,32,1024]{2,1,0:T(8,128)S(1)}, u32[]{:S(2)}, u32[]{:S(2)}) %collective-permute-start.13) | collective-permute-done | bytes 786464 | tf_op jit(solution)/shard_map/ppermute | solution.py:28
  258.6 0.9 copy-done.5
  259.4 14.6 %fusion.8 = f32[12,32,1024]{2,1,0:T(8,128)S(1)} fusion(f32[12,32,1024]{2,1,0:T(8,128)S(1)} %fusion.64, f32[12,32,192]{2,1,0:T(8,128)S(1)} %broadcast_multiply_fusion.1, f32[12,32,192]{2,1,0:T(8,128)S(1)} %broadcast_multiply_fusion.4, f32[12,6,1024]{2,1,0:T(8,128)S(1)} %broadcast_multiply_fusion.7, f32[12,6,1024]{2,1,0:T(8,128)S(1)} %broadcast_multiply_fusion.10, ...), kind=kLoop, calls=%fused_computation.189 | loop fusion | flops 33423360 | bytes 7471104 | tf_op jit(solution)/shard_map/div | solution.py:58
  274.0 4.5 reshape.45
  278.6 13.7 %fusion.246 = f32[32,64]{1,0:T(8,128)S(1)} fusion(f32[12288,32]{1,0:T(8,128)} %reshape.42, f32[64,12288]{1,0:T(8,128)} %bitcast.35), kind=kOutput, calls=%fused_computation.467 | convolution fusion | flops 301989888 | bytes 4726784 | tf_op jit(solution)/shard_map/cp,kcq->pkq/dot_general | solution.py:88
  292.4 10.0 fusion.247
  302.4 682.8 %all-reduce = (f32[32,64]{1,0:T(8,128)S(1)}, f32[32,64]{1,0:T(8,128)S(1)}) all-reduce(f32[32,64]{1,0:T(8,128)S(1)} %fusion.246, f32[32,64]{1,0:T(8,128)S(1)} %fusion.247), channel_id=1, replica_groups=mesh['dom'=128,'band'=2] {'dom'}, use_global_device_ids=true, to_apply=%region_0.1 | all-reduce | flops 4096 | bytes 32768 | tf_op jit(solution)/shard_map/psum | solution.py:94
  985.2 5.2 all_gather.10
  990.6 5.8 cholesky.17
  996.5 0.6 compare_reduce_fusion
  997.1 0.7 fusion.228
  997.8 4.9 custom-call.7
  1002.7 0.2 fusion.229
  1003.0 21.6 %convolution_bitcast_fusion = f32[12288,32]{1,0:T(8,128)} fusion(f32[2,12288,32]{1,2,0:T(8,128)S(1)} %copy-done, f32[2,32,32]{1,0,2:T(2,128)S(1)} %reshape.43), kind=kOutput, calls=%fused_computation | convolution fusion | flops 301989888 | bytes 4726784 | tf_op jit(solution)/shard_map/kcq,kqp->cp/dot_general | solution.py:111
  1024.6 5.9 reshape.44
  1030.5 3.3 all_gather.11
  1034.0 0.8 fusion.248
  (47 shorter events, 1.3 us)
Async XLA Ops:
  7.2 9.7 copy-start.2
  7.2 271.4 %all-gather.2.cloned.1.call-start = ((), (), s32[]{:S(2)}) async-start(), calls=%async_computation | async-start | bytes 4718592 | tf_op jit(solution)/shard_map/all_gather | solution.py:86
  9.5 34.5 %collective-permute-start.5 = (f32[12,32,192]{2,1,0:T(8,128)}, f32[12,32,192]{2,1,0:T(8,128)S(1)}, u32[]{:S(2)}, u32[]{:S(2)}) collective-permute-start(f32[12,32,192]{2,1,0:T(8,128)} %get-tuple-element.23), channel_id=1, source_target_pairs={{0,2},{2,4},{4,6},{6,8},{8,10},{10,12},{12,14},{14,16},{16,18},{18... | collective-permute-start | bytes 884744 | tf_op jit(solution)/shard_map/ppermute | solution.py:28
  14.9 32.2 %collective-permute-start.4 = (f32[12,32,192]{2,1,0:T(8,128)}, f32[12,32,192]{2,1,0:T(8,128)}, u32[]{:S(2)}, u32[]{:S(2)}) collective-permute-start(f32[12,32,192]{2,1,0:T(8,128)} %get-tuple-element.22), channel_id=1, source_target_pairs={{2,0},{4,2},{6,4},{8,6},{10,8},{12,10},{14,12},{16,14},{18,16},{20... | collective-permute-start | bytes 884744 | tf_op jit(solution)/shard_map/ppermute | solution.py:28
  17.8 31.1 %collective-permute-start.3 = (f32[12,6,1024]{2,1,0:T(8,128)}, f32[12,6,1024]{2,1,0:T(8,128)}, u32[]{:S(2)}, u32[]{:S(2)}) collective-permute-start(f32[12,6,1024]{2,1,0:T(8,128)} %get-tuple-element.21), channel_id=1, source_target_pairs={{0,8},{2,10},{4,12},{6,14},{8,16},{10,18},{12,20},{14,22},{16,24},... | collective-permute-start | bytes 884744 | tf_op jit(solution)/shard_map/ppermute | solution.py:28
  24.7 10.4 copy-start.9
  24.7 40.4 %collective-permute-start.2 = (f32[12,6,1024]{2,1,0:T(8,128)}, f32[12,6,1024]{2,1,0:T(8,128)}, u32[]{:S(2)}, u32[]{:S(2)}) collective-permute-start(f32[12,6,1024]{2,1,0:T(8,128)} %get-tuple-element.20), channel_id=1, source_target_pairs={{8,0},{10,2},{12,4},{14,6},{16,8},{18,10},{20,12},{22,14},{24,16},... | collective-permute-start | bytes 884744 | tf_op jit(solution)/shard_map/ppermute | solution.py:28
  27.4 48.1 %collective-permute-start.1 = (f32[6,32,1024]{2,1,0:T(8,128)}, f32[6,32,1024]{2,1,0:T(8,128)}, u32[]{:S(2)}, u32[]{:S(2)}) collective-permute-start(f32[6,32,1024]{2,1,0:T(8,128)} %get-tuple-element.19), channel_id=1, source_target_pairs={{0,32},{2,34},{4,36},{6,38},{8,40},{10,42},{12,44},{14,46},{16,48}... | collective-permute-start | bytes 2359304 | tf_op jit(solution)/shard_map/ppermute | solution.py:28
  43.9 31.6 %copy-start.3 = (f32[12,32,1024]{2,1,0:T(8,128)}, f32[12,32,1024]{2,1,0:T(8,128)S(1)}, u32[]{:S(2)}) copy-start(f32[12,32,1024]{2,1,0:T(8,128)S(1)} %mul.195) | copy-start | bytes 4718596
  43.9 0.8 copy-start.8
  44.8 30.7 %collective-permute-start = (f32[6,32,1024]{2,1,0:T(8,128)}, f32[6,32,1024]{2,1,0:T(8,128)}, u32[]{:S(2)}, u32[]{:S(2)}) collective-permute-start(f32[6,32,1024]{2,1,0:T(8,128)} %get-tuple-element.18), channel_id=1, source_target_pairs={{32,0},{34,2},{36,4},{38,6},{40,8},{42,10},{44,12},{46,14},{48,16}... | collective-permute-start | bytes 2359304 | tf_op jit(solution)/shard_map/ppermute | solution.py:28
  93.2 23.0 %collective-permute-start.11 = (f32[12,32,192]{2,1,0:T(8,128)S(1)}, f32[12,32,192]{2,1,0:T(8,128)S(1)}, u32[]{:S(2)}, u32[]{:S(2)}) collective-permute-start(f32[12,32,192]{2,1,0:T(8,128)S(1)} %get-tuple-element.17), channel_id=1, source_target_pairs={{0,2},{2,4},{4,6},{6,8},{8,10},{10,12},{12,14},{14,16},{16,18},{18... | collective-permute-start | bytes 884744 | tf_op jit(solution)/shard_map/ppermute | solution.py:28
  97.4 20.3 %collective-permute-start.10 = (f32[12,32,192]{2,1,0:T(8,128)S(1)}, f32[12,32,192]{2,1,0:T(8,128)S(1)}, u32[]{:S(2)}, u32[]{:S(2)}) collective-permute-start(f32[12,32,192]{2,1,0:T(8,128)S(1)} %get-tuple-element.16), channel_id=1, source_target_pairs={{2,0},{4,2},{6,4},{8,6},{10,8},{12,10},{14,12},{16,14},{18,16},{20... | collective-permute-start | bytes 884744 | tf_op jit(solution)/shard_map/ppermute | solution.py:28
  99.7 18.8 %collective-permute-start.9 = (f32[12,6,1024]{2,1,0:T(8,128)S(1)}, f32[12,6,1024]{2,1,0:T(8,128)S(1)}, u32[]{:S(2)}, u32[]{:S(2)}) collective-permute-start(f32[12,6,1024]{2,1,0:T(8,128)S(1)} %get-tuple-element.15), channel_id=1, source_target_pairs={{0,8},{2,10},{4,12},{6,14},{8,16},{10,18},{12,20},{14,22},{16,24},... | collective-permute-start | bytes 884744 | tf_op jit(solution)/shard_map/ppermute | solution.py:28
  101.1 40.9 %collective-permute-start.8 = (f32[12,6,1024]{2,1,0:T(8,128)S(1)}, f32[12,6,1024]{2,1,0:T(8,128)S(1)}, u32[]{:S(2)}, u32[]{:S(2)}) collective-permute-start(f32[12,6,1024]{2,1,0:T(8,128)S(1)} %get-tuple-element.14), channel_id=1, source_target_pairs={{8,0},{10,2},{12,4},{14,6},{16,8},{18,10},{20,12},{22,14},{24,16},... | collective-permute-start | bytes 884744 | tf_op jit(solution)/shard_map/ppermute | solution.py:28
  102.4 54.2 %collective-permute-start.7 = (f32[6,32,1024]{2,1,0:T(8,128)S(1)}, f32[6,32,1024]{2,1,0:T(8,128)S(1)}, u32[]{:S(2)}, u32[]{:S(2)}) collective-permute-start(f32[6,32,1024]{2,1,0:T(8,128)S(1)} %get-tuple-element.13), channel_id=1, source_target_pairs={{0,32},{2,34},{4,36},{6,38},{8,40},{10,42},{12,44},{14,46},{16,48}... | collective-permute-start | bytes 2359304 | tf_op jit(solution)/shard_map/ppermute | solution.py:28
  116.2 40.4 %collective-permute-start.6 = (f32[6,32,1024]{2,1,0:T(8,128)S(1)}, f32[6,32,1024]{2,1,0:T(8,128)S(1)}, u32[]{:S(2)}, u32[]{:S(2)}) collective-permute-start(f32[6,32,1024]{2,1,0:T(8,128)S(1)} %get-tuple-element.12), channel_id=1, source_target_pairs={{32,0},{34,2},{36,4},{38,6},{40,8},{42,10},{44,12},{46,14},{48,16}... | collective-permute-start | bytes 2359304 | tf_op jit(solution)/shard_map/ppermute | solution.py:28
  156.5 0.9 copy-start.6
  157.4 0.9 copy-start.7
  186.5 34.4 %collective-permute-start.17 = (f32[12,32,192]{2,1,0:T(8,128)}, f32[12,32,192]{2,1,0:T(8,128)}, u32[]{:S(2)}, u32[]{:S(2)}) collective-permute-start(f32[12,32,192]{2,1,0:T(8,128)} %get-tuple-element.11), channel_id=1, source_target_pairs={{0,2},{2,4},{4,6},{6,8},{8,10},{10,12},{12,14},{14,16},{16,18},{18... | collective-permute-start | bytes 884744 | tf_op jit(solution)/shard_map/ppermute | solution.py:28
  193.8 29.6 %collective-permute-start.16 = (f32[12,32,192]{2,1,0:T(8,128)S(1)}, f32[12,32,192]{2,1,0:T(8,128)}, u32[]{:S(2)}, u32[]{:S(2)}) collective-permute-start(f32[12,32,192]{2,1,0:T(8,128)S(1)} %get-tuple-element.10), channel_id=1, source_target_pairs={{2,0},{4,2},{6,4},{8,6},{10,8},{12,10},{14,12},{16,14},{18,16},{20... | collective-permute-start | bytes 884744 | tf_op jit(solution)/shard_map/ppermute | solution.py:28
  200.8 23.6 %collective-permute-start.15 = (f32[12,6,1024]{2,1,0:T(8,128)}, f32[12,6,1024]{2,1,0:T(8,128)S(1)}, u32[]{:S(2)}, u32[]{:S(2)}) collective-permute-start(f32[12,6,1024]{2,1,0:T(8,128)} %get-tuple-element.9), channel_id=1, source_target_pairs={{0,8},{2,10},{4,12},{6,14},{8,16},{10,18},{12,20},{14,22},{16,24},... | collective-permute-start | bytes 884744 | tf_op jit(solution)/shard_map/ppermute | solution.py:28
  202.1 30.4 %collective-permute-start.14 = (f32[12,6,1024]{2,1,0:T(8,128)}, f32[12,6,1024]{2,1,0:T(8,128)S(1)}, u32[]{:S(2)}, u32[]{:S(2)}) collective-permute-start(f32[12,6,1024]{2,1,0:T(8,128)} %get-tuple-element.8), channel_id=1, source_target_pairs={{8,0},{10,2},{12,4},{14,6},{16,8},{18,10},{20,12},{22,14},{24,16},... | collective-permute-start | bytes 884744 | tf_op jit(solution)/shard_map/ppermute | solution.py:28
  203.4 55.1 %collective-permute-start.13 = (f32[6,32,1024]{2,1,0:T(8,128)S(1)}, f32[6,32,1024]{2,1,0:T(8,128)S(1)}, u32[]{:S(2)}, u32[]{:S(2)}) collective-permute-start(f32[6,32,1024]{2,1,0:T(8,128)S(1)} %get-tuple-element.7), channel_id=1, source_target_pairs={{0,32},{2,34},{4,36},{6,38},{8,40},{10,42},{12,44},{14,46},{16,48}... | collective-permute-start | bytes 2359304 | tf_op jit(solution)/shard_map/ppermute | solution.py:28
  220.9 38.5 %copy-start.4 = (f32[12,32,1024]{2,1,0:T(8,128)S(1)}, f32[12,32,1024]{2,1,0:T(8,128)}, u32[]{:S(2)}) copy-start(f32[12,32,1024]{2,1,0:T(8,128)} %copy-done.3) | copy-start | bytes 4718596
  220.9 38.5 %collective-permute-start.12 = (f32[6,32,1024]{2,1,0:T(8,128)S(1)}, f32[6,32,1024]{2,1,0:T(8,128)}, u32[]{:S(2)}, u32[]{:S(2)}) collective-permute-start(f32[6,32,1024]{2,1,0:T(8,128)S(1)} %get-tuple-element.6), channel_id=1, source_target_pairs={{32,0},{34,2},{36,4},{38,6},{40,8},{42,10},{44,12},{46,14},{48,16}... | collective-permute-start | bytes 2359304 | tf_op jit(solution)/shard_map/ppermute | solution.py:28
  258.6 0.9 copy-start.5
  278.6 13.7 %copy-start = (f32[2,12288,32]{1,2,0:T(8,128)S(1)}, f32[2,12288,32]{1,2,0:T(8,128)}, u32[]{:S(2)}) copy-start(f32[2,12288,32]{1,2,0:T(8,128)} %all-gather.2.cloned.1.call-done) | copy-start | bytes 9437188
  278.6 13.7 %copy-start.1 = (f32[12288,32]{1,0:T(8,128)S(1)}, f32[12288,32]{1,0:T(8,128)}, u32[]{:S(2)}) copy-start(f32[12288,32]{1,0:T(8,128)} %reshape.45) | copy-start | bytes 4718596
Sparse Core Ops, SparseCore 0:
  186.6 73.8 all-gather.1
where the time goes:
time: 1060 us; the launch traced here: 1040 us
  blocking collectives  691 us (65%)
  waiting for transfers between devices  93.6 us (9%)
  starting transfers between devices  79.4 us (7%)
  other arithmetic  72.5 us (7%)
  matrix products  46.5 us (4%)
  local copies, waits for them, and re-layouts  43.9 us (4%)
  between operations  14.7 us (1%)
    psum x1, blocking collectives, local(): over_sum, hamt_sum = lax.psum((over_rows, ham_rows), 'dom')  683 us
    ppermute x18, waiting for transfers between devices, passed_along(): return lax.ppermute(x, axis, pairs)  93.5 us
    ppermute x18, starting transfers between devices, passed_along(): return lax.ppermute(x, axis, pairs)  79.4 us
    div x2, other arithmetic, scaled_operator(): (-0.5 / SPACING ** 2 * lap + potential_term - CENTER * field) / HALFWIDTH  32.1 us
    dot_general x1, matrix products, local(): jnp.einsum('kcq,kqp->cp', every_block, part_coeffs, precision=highest)  21.6 us
  transfers between devices with their start and end apart: 19, of which 6 were waited for; matrix products, arithmetic and copies ran while one was open for 4% of the time, Pallas kernels for 0%

commit v1 on v0

v1 whole, which is shorter than its diff:
```python
import functools

import jax
import jax.numpy as jnp
from jax import lax
from jax.experimental import pallas as pl
from jax.experimental.pallas import tpu as pltpu
from jax.sharding import PartitionSpec as P

COEFFS = (
    -5369.0 / 1800.0,
    12.0 / 7.0,
    -15.0 / 56.0,
    10.0 / 189.0,
    -1.0 / 112.0,
    2.0 / 1925.0,
    -1.0 / 16632.0,
)
SPACING = 0.32
CENTER = 71.0
HALFWIDTH = 69.0
KINETIC = -0.5 / SPACING**2 / HALFWIDTH
A = tuple(KINETIC * c for c in COEFFS)

CX, CY, CZ, OB = 12, 32, 32, 32
PX, PY, PZ = 8, 4, 4
NJ = CZ * OB // 128
CELLS = PX * CX * PY * CY * PZ * CZ
MESH = pl.DeviceIdType.MESH
HIGHEST = lax.Precision.HIGHEST
XO, JO, YO = 6, 2, 8
OWN = (pl.ds(XO, CX), pl.ds(JO, NJ), pl.ds(YO, CY))


def stencil(field, pot, x):
    lane = lax.broadcasted_iota(jnp.int32, (CY, 128), 1)

    def tile(j, dx=0, dy=0):
        return field[XO + x + dx, JO + j, pl.ds(YO + dy, CY), :]

    def partial(j):
        m2, m1, v, p1 = tile(j - 2), tile(j - 1), tile(j), tile(j + 1)
        t1 = A[3] * m1 + A[1] * v + A[5] * p1
        t2 = A[2] * (v + m1) + A[6] * (p1 + m2)
        t3 = A[3] * v + A[1] * m1 + A[5] * m2
        return (
            pltpu.roll(t1, 96, 1),
            pltpu.roll(t2, 64, 1),
            pltpu.roll(t3, 32, 1),
        )

    out = []
    low = partial(0)
    for j in range(NJ):
        high = partial(j + 1)
        acc = jnp.where(lane < 96, low[0], high[0])
        acc = acc + jnp.where(lane < 64, low[1], high[1])
        acc = acc + jnp.where(lane < 32, low[2], high[2])
        low = high
        acc = acc + pot[x, j] * tile(j)
        for k in range(1, 7):
            terms = tile(j, k) + tile(j, -k) + tile(j, 0, k) + tile(j, 0, -k)
            if k == 4:
                terms = terms + (tile(j + 1) + tile(j - 1))
            acc = acc + A[k] * terms
        out.append(acc)
    return out


def filter_kernel(
    orb_ref,
    pot_ref,
    filt_ref,
    band_ref,
    mats_ref,
    e0,
    e1,
    e2,
    img,
    pot,
    other,
    part,
    recv,
    load_sem,
    hs,
    hr,
    bs,
    br,
    rs,
    rr,
):
    dom = lax.axis_index("dom")
    band = lax.axis_index("band")
    tz = lax.rem(dom, PZ)
    ty = lax.rem(dom // PZ, PY)
    tx = dom // (PY * PZ)
    px, py, pz, core = dom // 32, lax.rem(dom // 8, 4), lax.rem(dom // 2, 4), lax.rem(dom, 2)

    loads = [
        pltpu.make_async_copy(
            orb_ref.at[0, 0, :, :, pl.ds(128 * j, 128)],
            e0.at[pl.ds(XO, CX), JO + j, pl.ds(YO, CY)],
            load_sem.at[j],
        )
        for j in range(NJ)
    ]
    for copy in loads:
        copy.start()

    def place(x, y, z, c):
        return ((x * 4 + y) * 4 + z) * 2 + c

    faces = (
        (PY * PZ, tx, PX),
        (PZ, ty, PY),
        (1, tz, PZ),
    )
    peers = [(place(px, py, pz, 1 - core), band), (dom, 1 - band)]
    zpeers = [(place(px, py, lax.rem(pz + k, 4), core), band) for k in range(1, 4)]
    ypeers = [(place(px, lax.rem(py + k, 4), pz, core), band) for k in range(1, 4)]
    xpeers = [(place(lax.rem(px + k, 4), py, pz, core), band) for k in range(1, 4)]

    barrier = pltpu.get_barrier_semaphore()
    count = jnp.int32(11)
    for peer in peers + zpeers + ypeers + xpeers:
        pl.semaphore_signal(barrier, inc=1, device_id=peer, device_id_type=MESH)
    for stride, at, n in faces:
        has_low, has_high = at > 0, at < n - 1
        count = count + has_low.astype(jnp.int32) + has_high.astype(jnp.int32)

        @pl.when(has_low)
        def _():
            pl.semaphore_signal(barrier, inc=1, device_id=(dom - stride, band), device_id_type=MESH)

        @pl.when(has_high)
        def _():
            pl.semaphore_signal(barrier, inc=1, device_id=(dom + stride, band), device_id_type=MESH)

    row = lax.broadcasted_iota(jnp.int32, (CZ, CZ * OB), 0)
    col = lax.broadcasted_iota(jnp.int32, (CZ, CZ * OB), 1)
    spread = (row == col // OB).astype(jnp.float32)

    def spread_pot(x, carry):
        scaled = (pot_ref[0, x] - CENTER) * (1.0 / HALFWIDTH) + 3.0 * A[0]
        wide = jnp.dot(scaled, spread, precision=HIGHEST, preferred_element_type=jnp.float32)
        for j in range(NJ):
            pot[x, j] = wide[:, 128 * j : 128 * (j + 1)]
        return carry

    pl.semaphore_wait(barrier, count)

    def sections(dim):
        sizes = ((XO, CX, 6), (JO, NJ, 2), (YO, CY, 8))
        axis = (0, 2, 1)[dim]
        start, extent, depth = sizes[axis]
        picks = []
        for at in (start, start + extent - depth, start - depth, start + extent):
            index = list(OWN)
            index[axis] = pl.ds(at, depth)
            picks.append(tuple(index))
        return picks

    def halo(field, step):
        copies = []
        for dim, (stride, at, n) in enumerate(faces):
            low_rim, high_rim, below, above = sections(dim)
            up = pltpu.make_async_remote_copy(
                field.at[high_rim],
                field.at[below],
                hs.at[step, 2 * dim],
                hr.at[step, 2 * dim],
                device_id=(lax.rem(dom + stride, 128), band),
                device_id_type=MESH,
            )
            down = pltpu.make_async_remote_copy(
                field.at[low_rim],
                field.at[above],
                hs.at[step, 2 * dim + 1],
                hr.at[step, 2 * dim + 1],
                device_id=(lax.rem(dom - stride + 128, 128), band),
                device_id_type=MESH,
            )
            copies.append((up, at < n - 1, at > 0, below))
            copies.append((down, at > 0, at < n - 1, above))
        return copies

    def start(copies, field):
        for copy, sends, receives, landing in copies:

            @pl.when(sends)
            def _():
                copy.start()

        for copy, sends, receives, landing in copies:

            @pl.when(jnp.logical_not(receives))
            def _():
                xs, js, ys = landing

                def clear(i, carry):
                    field[xs.start + i, js, ys] = jnp.zeros((js.size, ys.size, 128), jnp.float32)
                    return carry

                lax.fori_loop(0, xs.size, clear, 0)

    def arrive(copies):
        for copy, sends, receives, landing in copies:

            @pl.when(receives)
            def _():
                copy.wait_recv()

    def drain(copies):
        for copy, sends, receives, landing in copies:

            @pl.when(sends)
            def _():
                copy.wait_send()

    for copy in loads:
        copy.wait()
    first = halo(e0, 0)
    start(first, e0)
    lax.fori_loop(0, CX, spread_pot, 0)
    arrive(first)

    def step_one(x, carry):
        for j, value in enumerate(stencil(e0, pot, x)):
            e1[XO + x, JO + j, pl.ds(YO, CY), :] = value
        return carry

    lax.fori_loop(0, CX, step_one, 0)
    second = halo(e1, 1)
    start(second, e1)
    arrive(second)

    def step_two(x, carry):
        for j, value in enumerate(stencil(e1, pot, x)):
            own = e0[XO + x, JO + j, pl.ds(YO, CY), :]
            e2[XO + x, JO + j, pl.ds(YO, CY), :] = 2.0 * value - own
        return carry

    lax.fori_loop(0, CX, step_two, 0)
    third = halo(e2, 2)
    start(third, e2)
    over = pltpu.make_async_remote_copy(
        e2.at[OWN], other, bs, br, device_id=(dom, 1 - band), device_id_type=MESH
    )

    @pl.when(band == 0)
    def _():
        over.start()

    keep = pltpu.make_async_copy(e2.at[OWN], filt_ref, load_sem.at[0])
    keep.start()
    drain(first)
    drain(second)
    arrive(third)

    def step_three(x, carry):
        for j, value in enumerate(stencil(e2, pot, x)):
            img[x, j] = value
        return carry

    lax.fori_loop(0, CX, step_three, 0)

    @pl.when(band == 1)
    def _():
        over.wait_recv()

    def gram(left):
        def add(x, acc):
            rows = left(x)
            own = e2[XO + x, pl.ds(JO, NJ), pl.ds(YO, CY), :].reshape(NJ * CY, 128)
            both = jnp.concatenate([own, img[x].reshape(NJ * CY, 128)], axis=1)
            return acc + lax.dot_general(
                rows,
                both,
                (((0,), (0,)), ((), ())),
                precision=HIGHEST,
                preferred_element_type=jnp.float32,
            )

        acc = lax.fori_loop(0, CX, add, jnp.zeros((128, 256), jnp.float32))
        blocks = []
        for half in range(2):
            total = acc[:OB, 128 * half : 128 * half + OB]
            for g in range(1, 4):
                total = total + acc[OB * g : OB * (g + 1), 128 * half + OB * g : 128 * half + OB * (g + 1)]
            blocks.append(total)
        return blocks

    part[...] = jnp.zeros_like(part)

    @pl.when(band == 0)
    def _():
        corr, ham = gram(
            lambda x: e2[XO + x, pl.ds(JO, NJ), pl.ds(YO, CY), :].reshape(NJ * CY, 128)
        )
        part[0, 0, :, 0:OB] = corr
        part[0, 0, :, 2 * OB : 3 * OB] = ham

    @pl.when(band == 1)
    def _():
        corr, ham = gram(
            lambda x: e2[XO + x, pl.ds(JO, NJ), pl.ds(YO, CY), :].reshape(NJ * CY, 128)
        )
        part[0, 1, :, OB : 2 * OB] = corr
        part[0, 1, :, 3 * OB : 4 * OB] = ham
        corr, ham = gram(lambda x: other[x].reshape(NJ * CY, 128))
        part[0, 0, :, OB : 2 * OB] = corr
        part[0, 0, :, 3 * OB : 4 * OB] = ham

    keep.wait()
    back = pltpu.make_async_copy(other, band_ref, load_sem.at[1])

    @pl.when(band == 1)
    def _():
        back.start()

    def exchange(source, targets, slot):
        copies = []
        for k, peer in enumerate(targets):
            copy = pltpu.make_async_remote_copy(
                source,
                recv.at[slot + k],
                rs.at[slot + k],
                rr.at[slot + k],
                device_id=peer,
                device_id_type=MESH,
            )
            copy.start()
            copies.append(copy)
        for copy in copies:
            copy.wait()

    exchange(part.at[0, 1 - core], [peers[0]], 0)
    part[1, 0] = part[0, core] + recv[0]
    exchange(part.at[1, 0], [peers[1]], 1)
    part[1, 1] = part[1, 0] + recv[1]
    exchange(part.at[1, 1], zpeers, 2)
    part[2, 0] = part[1, 1] + recv[2] + recv[3] + recv[4]
    exchange(part.at[2, 0], ypeers, 5)
    part[2, 1] = part[2, 0] + recv[5] + recv[6] + recv[7]
    exchange(part.at[2, 1], xpeers, 8)
    part[3, 0] = part[2, 1] + recv[8] + recv[9] + recv[10]
    exchange(part.at[3, 0], [peers[0]], 11)
    mats_ref[core] = part[3, 0]
    mats_ref[1 - core] = recv[11]

    drain(third)

    @pl.when(band == 0)
    def _():
        over.wait_send()

    @pl.when(band == 1)
    def _():
        back.wait()


def run_filter(orbitals, potential):
    big = (XO * 2 + CX, JO * 2 + NJ, YO * 2 + CY, 128)
    tile = (CX, NJ, CY, 128)
    vmem = pl.BlockSpec(memory_space=pltpu.VMEM)
    hbm = pl.BlockSpec(memory_space=pl.ANY)
    f32 = jnp.float32
    dma = pltpu.SemaphoreType.DMA
    return pl.pallas_call(
        filter_kernel,
        out_shape=(
            jax.ShapeDtypeStruct(tile, f32),
            jax.ShapeDtypeStruct(tile, f32),
            jax.ShapeDtypeStruct((2, OB, 128), f32),
        ),
        in_specs=[hbm, vmem],
        out_specs=(hbm, hbm, vmem),
        scratch_shapes=[
            pltpu.VMEM(big, f32),
            pltpu.VMEM(big, f32),
            pltpu.VMEM(big, f32),
            pltpu.VMEM(tile, f32),
            pltpu.VMEM(tile, f32),
            pltpu.VMEM(tile, f32),
            pltpu.VMEM((4, 2, OB, 128), f32),
            pltpu.VMEM((12, OB, 128), f32),
            dma((NJ,)),
            dma((3, 6)),
            dma((3, 6)),
            dma,
            dma,
            dma((12,)),
            dma((12,)),
        ],
        compiler_params=pltpu.CompilerParams(
            collective_id=0, has_side_effects=True, vmem_limit_bytes=48 << 20
        ),
    )(orbitals, potential)


def rotate_kernel(own_ref, other_ref, coef_ref, out_ref):
    band = lax.axis_index("band")
    own = own_ref[...].reshape(CX * CY, 128)
    mine = jnp.dot(own, coef_ref[0], precision=HIGHEST, preferred_element_type=jnp.float32)

    @pl.when(band == 0)
    def _():
        out_ref[0, 0] = mine.reshape(CX, CY, 128)

    @pl.when(band == 1)
    def _():
        rest = other_ref[...].reshape(CX * CY, 128)
        total = mine + jnp.dot(
            rest, coef_ref[1], precision=HIGHEST, preferred_element_type=jnp.float32
        )
        out_ref[0, 0] = total.reshape(CX, CY, 128)


def rotate(own, other, coef):
    spec = pl.BlockSpec((CX, 1, CY, 128), lambda j: (0, j, 0, 0))
    return pl.pallas_call(
        rotate_kernel,
        out_shape=jax.ShapeDtypeStruct((1, 1, CX, CY, CZ * OB), jnp.float32),
        grid=(NJ,),
        in_specs=[spec, spec, pl.BlockSpec((2, 128, 128), lambda j: (0, 0, 0))],
        out_specs=pl.BlockSpec((1, 1, CX, CY, 128), lambda j: (0, 0, 0, 0, j)),
    )(own, other, coef)


def local(orbitals, potential):
    filt, other, mats = run_filter(orbitals, potential)
    mats = mats.reshape(2 * OB, 128) / CELLS
    corr, ham = mats[:, : 2 * OB], mats[:, 2 * OB :]

    def whole(m):
        return jnp.block([[m[:OB, :OB], m[:OB, OB:]], [m[:OB, OB:].T, m[OB:, OB:]]])

    corr, ham = whole(corr), whole(ham)
    lower = jnp.linalg.cholesky(corr)
    inverse = lax.linalg.triangular_solve(
        lower, jnp.eye(2 * OB, dtype=jnp.float32), left_side=True, lower=True
    )
    projected = jnp.dot(jnp.dot(inverse, ham, precision=HIGHEST), inverse.T, precision=HIGHEST)
    band = lax.axis_index("band")
    rows = lax.dynamic_slice_in_dim(inverse, band * OB, OB, 0)
    mine = lax.dynamic_slice_in_dim(rows, band * OB, OB, 1).T
    rest = rows[:, :OB].T
    eye = jnp.eye(4, dtype=jnp.float32)
    coef = jnp.stack([jnp.kron(eye, mine), jnp.kron(eye, rest)])
    return rotate(filt, other, coef), projected


def solution(mesh):
    return jax.shard_map(
        local,
        mesh=mesh,
        in_specs=(P("dom", "band", None, None, None), P("dom", None, None, None)),
        out_specs=(P("dom", "band", None, None, None), P()),
        check_vma=False,
    )
```

time: 1060 us -> 248 us (0.23); the launches traced: 1040 us -> 246 us
  blocking collectives: 691 us -> 0 us
  Pallas kernels: 0 us -> 226 us
  waiting for transfers between devices: 93.6 us -> 0 us
  starting transfers between devices: 79.4 us -> 0 us
  other arithmetic: 72.5 us -> 13.1 us
  matrix products: 46.5 us -> 1.26 us
  local copies, waits for them, and re-layouts: 43.9 us -> 5.64 us
  between operations: 14.7 us -> 0.72 us
    psum x1 -> x0, blocking collectives: 683 us -> none  [local(): over_sum, hamt_sum = lax.psum((over_rows, ham_rows), 'dom')]
    pallas_call x0 -> x2, Pallas kernels: none -> 226 us  [the longest x1 217 us: run_filter(): pl.pallas_call(filter_kernel, out_shape=(jax.ShapeDtypeStruct(tile, f32),...]
    ppermute x18 -> x0, waiting for transfers between devices: 93.5 us -> none  [passed_along(): return lax.ppermute(x, axis, pairs)]
    ppermute x18 -> x0, starting transfers between devices: 79.4 us -> none  [passed_along(): return lax.ppermute(x, axis, pairs)]
    dot_general x5 -> x2, matrix products: 46.3 us -> 1.03 us  [the longest x1 0.8 us: local(): jnp.dot(jnp.dot(inverse, ham, precision=HIGHEST), inverse.T, precision=HI...]
    div x4 -> x2, other arithmetic: 32.1 us -> 0.1 us  [the longest x1 0.09 us: local(): lower = jnp.linalg.cholesky(corr)]
    sub x1 -> x0, other arithmetic: 17.4 us -> none  [local(): filtered = 2.0 * scaled_operator(first, pot_tile, valid) - field]
    reshape x4 -> x0, local copies, waits for them, and re-layouts: 14.6 us -> none  [the longest x1 5.9 us: local(): return (rotated.reshape(1, 1, cx, cy, zo), projected)]
  transfers between devices with their start and end apart: 19 -> 0, of which waited for: 6 -> 0; matrix products, arithmetic and copies ran while one was open for 4% -> 0% of each run, Pallas kernels for 0% -> 0%
where the time goes in v1:
time: 248 us; the launch traced here: 246 us
  Pallas kernels  226 us (91%)
  other arithmetic  13.1 us (5%)
  local copies, waits for them, and re-layouts  5.64 us (2%)
    pallas_call x1, Pallas kernels, run_filter(): pl.pallas_call(filter_kernel, out_shape=(jax.ShapeDtypeStruct(tile, f32),...  217 us
    pallas_call x1, Pallas kernels, rotate(): pl.pallas_call(rotate_kernel, out_shape=jax.ShapeDtypeStruct((1, 1, CX, C...  8.39 us
    another operation x3, other arithmetic, local(): lower = jnp.linalg.cholesky(corr)  6.53 us
    another operation x2, other arithmetic, local(): lax.linalg.triangular_solve(lower, jnp.eye(2 * OB, dtype=jnp.float32), le...  5.55 us

profile of v1, /device:TPU:33, one launch (start us, length us, event | category | flops | bytes accessed | tf_op | source)
XLA Modules:
  0.0 246.5 jit_solution(15910575418980029416)
XLA Ops:
  0.6 0.0 copy-start
  0.7 1.4 copy-done
  2.1 0.0 copy-start.3
  2.1 0.9 copy-done.3
  3.0 217.4 %shard_map.41 = (f32[12,8,32,128]{3,2,1,0:T(8,128)S(1)}, f32[12,8,32,128]{3,2,1,0:T(8,128)S(1)}, f32[2,32,128]{2,1,0:T(8,128)S(1)}) custom-call(f32[1,1,12,32,1024]{4,3,2,1,0:T(8,128)S(1)} %copy-done, f32[1,12,32,32]{3,2,1,0:T(8,128)S(1)} %copy-done.3), custom_call_target="tpu_custom_call" | custom-call | tf_op jit(solution)/shard_map/pallas_call | solution.py:369
  220.4 0.0 copy-start.1
  220.4 1.2 copy-done.1
  221.6 0.0 copy-start.2
  221.6 1.2 copy-done.2
  222.7 0.1 fusion.12
  222.8 0.1 copy.16
  222.9 0.1 fusion.13
  222.9 0.1 copy.18
  223.0 0.1 copy.17
  223.1 0.1 maximum_maximum_fusion
  223.2 0.1 copy.12
  223.3 0.1 fusion.9
  223.4 5.9 %cholesky.17 = f32[64,64]{1,0:T(8,128)S(1)} custom-call(f32[64,64]{1,0:T(8,128)S(1)} %fusion.9), custom_call_target="Cholesky" | custom-call | tf_op jit(solution)/shard_map/jit(cholesky)/cholesky | solution.py:439
  229.2 0.6 compare_reduce_fusion
  229.9 0.7 fusion
  230.5 4.9 %custom-call.6 = f32[1,64,64]{1,2,0:T(8,128)S(1)} custom-call(f32[1,64,64]{2,1,0:T(8,128)S(1)} %fusion), custom_call_target="InvertDiagBlocksLowerTriangular" | custom-call | tf_op jit(solution)/shard_map/triangular_solve | solution.py:440
  235.4 0.2 fusion.7
  235.7 0.2 fusion.1
  235.9 0.8 fusion.14
  236.7 0.1 dynamic-slice_bitcast_fusion.1
  236.8 0.1 copy.13
  236.9 0.1 copy.14
  236.9 0.1 broadcast_multiply_fusion.1
  237.1 0.2 mul.61
  237.3 0.2 mul.64
  237.4 0.7 pad_maximum_fusion.coef_ref
  238.1 8.4 %shard_map.42 = f32[1,1,12,32,1024]{4,3,2,1,0:T(8,128)} custom-call(f32[12,8,32,128]{3,2,1,0:T(8,128)} %copy-done.1, f32[12,8,32,128]{3,2,1,0:T(8,128)} %copy-done.2, f32[2,128,128]{2,1,0:T(8,128)} %pad_maximum_fusion.coef_ref), custom_call_target="tpu_custom_call" | custom-call | tf_op jit(solution)/shard_map/pallas_call | solution.py:421
  (3 shorter events, 0.0 us)
Async XLA Ops:
  0.6 1.4 copy-start
  2.1 0.9 copy-start.3
  220.4 1.2 copy-start.1
  221.6 1.2 copy-start.2

commit v2 on v1

v2 whole, which is shorter than its diff:
```python
import functools

import jax
import jax.numpy as jnp
from jax import lax
from jax.experimental import pallas as pl
from jax.experimental.pallas import tpu as pltpu
from jax.sharding import PartitionSpec as P

COEFFS = (
    -5369.0 / 1800.0,
    12.0 / 7.0,
    -15.0 / 56.0,
    10.0 / 189.0,
    -1.0 / 112.0,
    2.0 / 1925.0,
    -1.0 / 16632.0,
)
SPACING = 0.32
CENTER = 71.0
HALFWIDTH = 69.0
KINETIC = -0.5 / SPACING**2 / HALFWIDTH
A = tuple(KINETIC * c for c in COEFFS)

CX, CY, CZ, OB = 12, 32, 32, 32
PX, PY, PZ = 8, 4, 4
NJ = CZ * OB // 128
CELLS = PX * CX * PY * CY * PZ * CZ
MESH = pl.DeviceIdType.MESH
HIGHEST = lax.Precision.HIGHEST
XO, JO, YO = 6, 2, 8
OWN = (pl.ds(XO, CX), pl.ds(JO, NJ), pl.ds(YO, CY))


def stencil(field, pot, x):
    lane = lax.broadcasted_iota(jnp.int32, (CY, 128), 1)

    def tile(j, dx=0, dy=0):
        return field[XO + x + dx, JO + j, pl.ds(YO + dy, CY), :]

    def partial(j):
        m2, m1, v, p1 = tile(j - 2), tile(j - 1), tile(j), tile(j + 1)
        t1 = A[3] * m1 + A[1] * v + A[5] * p1
        t2 = A[2] * (v + m1) + A[6] * (p1 + m2)
        t3 = A[3] * v + A[1] * m1 + A[5] * m2
        return (
            pltpu.roll(t1, 96, 1),
            pltpu.roll(t2, 64, 1),
            pltpu.roll(t3, 32, 1),
        )

    out = []
    low = partial(0)
    for j in range(NJ):
        high = partial(j + 1)
        acc = jnp.where(lane < 96, low[0], high[0])
        acc = acc + jnp.where(lane < 64, low[1], high[1])
        acc = acc + jnp.where(lane < 32, low[2], high[2])
        low = high
        acc = acc + pot[x, j] * tile(j)
        for k in range(1, 7):
            terms = tile(j, k) + tile(j, -k) + tile(j, 0, k) + tile(j, 0, -k)
            if k == 4:
                terms = terms + (tile(j + 1) + tile(j - 1))
            acc = acc + A[k] * terms
        out.append(acc)
    return out


def filter_kernel(
    orb_ref,
    pot_ref,
    out_ref,
    proj_ref,
    e0,
    e1,
    e2,
    img,
    pot,
    other,
    part,
    recv,
    work,
    coef,
    load_sem,
    hs,
    hr,
    bs,
    br,
    rs,
    rr,
):
    dom = lax.axis_index("dom")
    band = lax.axis_index("band")
    tz = lax.rem(dom, PZ)
    ty = lax.rem(dom // PZ, PY)
    tx = dom // (PY * PZ)
    px, py, pz, core = dom // 32, lax.rem(dom // 8, 4), lax.rem(dom // 2, 4), lax.rem(dom, 2)

    loads = [
        pltpu.make_async_copy(
            orb_ref.at[0, 0, :, :, pl.ds(128 * j, 128)],
            e0.at[pl.ds(XO, CX), JO + j, pl.ds(YO, CY)],
            load_sem.at[j],
        )
        for j in range(NJ)
    ]
    for copy in loads:
        copy.start()

    def place(x, y, z, c):
        return ((x * 4 + y) * 4 + z) * 2 + c

    faces = (
        (PY * PZ, tx, PX),
        (PZ, ty, PY),
        (1, tz, PZ),
    )
    twin = (place(px, py, pz, 1 - core), band)
    column = [
        (place(px, py, lax.rem(pz + k, 4), core), lax.rem(band + b, 2))
        for k in range(4)
        for b in range(2)
        if k or b
    ]
    plane = [
        (place(lax.rem(px + i, 4), lax.rem(py + k, 4), pz, core), band)
        for i in range(4)
        for k in range(4)
        if i or k
    ]
    stages = ((twin,), column, plane, (twin,))
    slots = (0, 1, 8, 23)

    barrier = pltpu.get_barrier_semaphore()
    count = jnp.int32(23)
    for peer in [twin] + column + plane:
        pl.semaphore_signal(barrier, inc=1, device_id=peer, device_id_type=MESH)
    for stride, at, n in faces:
        has_low, has_high = at > 0, at < n - 1
        count = count + has_low.astype(jnp.int32) + has_high.astype(jnp.int32)

        @pl.when(has_low)
        def _():
            pl.semaphore_signal(barrier, inc=1, device_id=(dom - stride, band), device_id_type=MESH)

        @pl.when(has_high)
        def _():
            pl.semaphore_signal(barrier, inc=1, device_id=(dom + stride, band), device_id_type=MESH)

    row = lax.broadcasted_iota(jnp.int32, (CZ, CZ * OB), 0)
    col = lax.broadcasted_iota(jnp.int32, (CZ, CZ * OB), 1)
    spread = (row == col // OB).astype(jnp.float32)

    def spread_pot(x, carry):
        scaled = (pot_ref[0, x] - CENTER) * (1.0 / HALFWIDTH) + 3.0 * A[0]
        wide = jnp.dot(scaled, spread, precision=HIGHEST, preferred_element_type=jnp.float32)
        for j in range(NJ):
            pot[x, j] = wide[:, 128 * j : 128 * (j + 1)]
        return carry

    pl.semaphore_wait(barrier, count)

    def sections(dim):
        sizes = ((XO, CX, 6), (JO, NJ, 2), (YO, CY, 6))
        axis = (0, 2, 1)[dim]
        start, extent, depth = sizes[axis]
        picks = []
        for at in (start, start + extent - depth, start - depth, start + extent):
            index = list(OWN)
            index[axis] = pl.ds(at, depth)
            picks.append(tuple(index))
        return picks

    def halo(field, step):
        copies = []
        for dim, (stride, at, n) in enumerate(faces):
            low_rim, high_rim, below, above = sections(dim)
            up = pltpu.make_async_remote_copy(
                field.at[high_rim],
                field.at[below],
                hs.at[step, 2 * dim],
                hr.at[step, 2 * dim],
                device_id=(lax.rem(dom + stride, 128), band),
                device_id_type=MESH,
            )
            down = pltpu.make_async_remote_copy(
                field.at[low_rim],
                field.at[above],
                hs.at[step, 2 * dim + 1],
                hr.at[step, 2 * dim + 1],
                device_id=(lax.rem(dom - stride + 128, 128), band),
                device_id_type=MESH,
            )
            copies.append((up, at < n - 1, at > 0, below))
            copies.append((down, at > 0, at < n - 1, above))
        return copies

    def start(copies, field):
        for copy, sends, receives, landing in copies:

            @pl.when(sends)
            def _():
                copy.start()

        for copy, sends, receives, landing in copies:

            @pl.when(jnp.logical_not(receives))
            def _():
                xs, js, ys = landing

                def clear(i, carry):
                    field[xs.start + i, js, ys] = jnp.zeros((js.size, ys.size, 128), jnp.float32)
                    return carry

                lax.fori_loop(0, xs.size, clear, 0)

    def arrive(copies):
        for copy, sends, receives, landing in copies:

            @pl.when(receives)
            def _():
                copy.wait_recv()

    def drain(copies):
        for copy, sends, receives, landing in copies:

            @pl.when(sends)
            def _():
                copy.wait_send()

    for copy in loads:
        copy.wait()
    first = halo(e0, 0)
    start(first, e0)
    lax.fori_loop(0, CX, spread_pot, 0)
    arrive(first)

    def step_one(x, carry):
        for j, value in enumerate(stencil(e0, pot, x)):
            e1[XO + x, JO + j, pl.ds(YO, CY), :] = value
        return carry

    lax.fori_loop(0, CX, step_one, 0)
    second = halo(e1, 1)
    start(second, e1)
    arrive(second)

    def step_two(x, carry):
        for j, value in enumerate(stencil(e1, pot, x)):
            own = e0[XO + x, JO + j, pl.ds(YO, CY), :]
            e2[XO + x, JO + j, pl.ds(YO, CY), :] = 2.0 * value - own
        return carry

    lax.fori_loop(0, CX, step_two, 0)
    low, high = pl.ds(0, CX // 2), pl.ds(CX // 2, CX // 2)
    partner = (dom, 1 - band)

    def across(planes, at):
        return pltpu.make_async_remote_copy(
            e2.at[pl.ds(XO + planes.start, planes.size), OWN[1], OWN[2]],
            other.at[planes],
            bs.at[at],
            br.at[at],
            device_id=partner,
            device_id_type=MESH,
        )

    upper, lower, rest = across(high, 0), across(low, 1), across(low, 2)

    @pl.when(band == 0)
    def _():
        upper.start()

    @pl.when(band == 1)
    def _():
        lower.start()

    third = halo(e2, 2)
    start(third, e2)

    def own(x):
        return e2[XO + x, pl.ds(JO, NJ), pl.ds(YO, CY), :].reshape(NJ * CY, 128)

    def theirs(x):
        return other[x].reshape(NJ * CY, 128)

    def image(x):
        return img[x].reshape(NJ * CY, 128)

    def gram(left, right, begin, end):
        def add(x, acc):
            return acc + lax.dot_general(
                left(x),
                right(x),
                (((0,), (0,)), ((), ())),
                precision=HIGHEST,
                preferred_element_type=jnp.float32,
            )

        acc = lax.fori_loop(begin, end, add, jnp.zeros((128, 128), jnp.float32))
        total = acc[:OB, :OB]
        for g in range(1, 4):
            total = total + acc[OB * g : OB * (g + 1), OB * g : OB * (g + 1)]
        return total

    def stage_copies(which, n):
        source = part.at[which, 0, 1 - core] if n == 0 else part.at[which, n, 0]
        return [
            pltpu.make_async_remote_copy(
                source,
                recv.at[which, slots[n] + k],
                rs.at[which, slots[n] + k],
                rr.at[which, slots[n] + k],
                device_id=peer,
                device_id_type=MESH,
            )
            for k, peer in enumerate(stages[n])
        ]

    def send(which, n):
        copies = stage_copies(which, n)
        for copy in copies:
            copy.start()
        return copies

    def collect(which, n, copies):
        for copy in copies:
            copy.wait()
        total = part[which, 0, core] if n == 0 else part[which, n, 0]
        if n == 3:
            part[which, 0, core] = total
            part[which, 0, 1 - core] = recv[which, slots[3]]
            return
        for k in range(len(copies)):
            total = total + recv[which, slots[n] + k]
        part[which, n + 1, 0] = total

    def put(which, column, block):
        for half in range(2):
            part[which, 0, half, :, OB * column : OB * (column + 1)] = block[
                half * (OB // 2) : (half + 1) * (OB // 2)
            ]

    part[...] = jnp.zeros_like(part)
    mine = gram(own, own, 0, CX)

    @pl.when(band == 0)
    def _():
        put(0, 0, mine)
        upper.wait_send()
        rest.start()
        lower.wait_recv()
        put(0, 1, gram(own, theirs, 0, CX // 2))

    @pl.when(band == 1)
    def _():
        put(0, 2, mine)
        upper.wait_recv()
        put(0, 1, gram(theirs, own, CX // 2, CX))

    for n in range(4):
        collect(0, n, send(0, n))

    eye = (
        lax.broadcasted_iota(jnp.int32, (OB, OB), 0) == lax.broadcasted_iota(jnp.int32, (OB, OB), 1)
    ).astype(jnp.float32)

    def matrix(which, dst):
        blocks = part[which, 0].reshape(OB, 128) * (1.0 / CELLS)
        cross = blocks[:, OB : 2 * OB]
        dst[0:OB, 0:OB] = blocks[:, 0:OB]
        dst[0:OB, OB : 2 * OB] = cross
        dst[OB : 2 * OB, OB : 2 * OB] = blocks[:, 2 * OB : 3 * OB]
        dst[OB : 2 * OB, 0:OB] = lax.dot_general(
            cross,
            eye,
            (((0,), (0,)), ((), ())),
            precision=HIGHEST,
            preferred_element_type=jnp.float32,
        )

    n_orb = 2 * OB
    row_id = lax.broadcasted_iota(jnp.int32, (n_orb, 128), 0)
    lane_id = lax.broadcasted_iota(jnp.int32, (n_orb, 128), 1)
    work[0] = (lane_id == row_id + n_orb).astype(jnp.float32)
    matrix(0, work.at[0])

    def eliminate(k, m):
        pivot_row = jnp.sum(jnp.where(row_id == k, m, 0.0), axis=0, keepdims=True)
        pivot_col = jnp.sum(jnp.where(lane_id == k, m, 0.0), axis=1, keepdims=True)
        pivot = jnp.sum(jnp.where(lane_id[:1] == k, pivot_row, 0.0), axis=1, keepdims=True)
        factor = jnp.where(row_id > k, pivot_col * (1.0 / pivot), 0.0)
        return m - factor * pivot_row

    m = lax.fori_loop(0, n_orb, eliminate, work[0])
    diag = jnp.sum(jnp.where(lane_id == row_id, m, 0.0), axis=1, keepdims=True)
    inverse = m * (1.0 / jnp.sqrt(diag))
    work[0] = inverse

    src = lax.broadcasted_iota(jnp.int32, (128, 128), 0)
    dst = lax.broadcasted_iota(jnp.int32, (128, 128), 1)
    same = src // OB == dst // OB
    mine_rows = work[0, pl.ds(pl.multiple_of(band * OB, OB), OB), :]

    def weights(column):
        pick = (src == n_orb + OB * column + lax.rem(dst, OB)).astype(jnp.float32)
        wide = jnp.dot(mine_rows, pick, precision=HIGHEST, preferred_element_type=jnp.float32)
        return jnp.where(same, jnp.concatenate([wide] * 4, axis=0), 0.0)

    coef[0] = weights(band)
    coef[1] = weights(0)

    arrive(third)

    def step_three(x, carry):
        for j, value in enumerate(stencil(e2, pot, x)):
            img[x, j] = value
        return carry

    lax.fori_loop(0, CX, step_three, 0)
    ham = gram(own, image, 0, CX)

    @pl.when(band == 0)
    def _():
        put(1, 0, ham)

    @pl.when(band == 1)
    def _():
        put(1, 2, ham)
        rest.wait_recv()
        put(1, 1, gram(theirs, image, 0, CX))

    def turn(x, carry):
        def times(rows, w):
            return lax.dot_general(
                rows,
                w,
                (((1,), (1,)), ((), ())),
                precision=HIGHEST,
                preferred_element_type=jnp.float32,
            )

        img[x] = times(own(x), coef[0]).reshape(NJ, CY, 128)

        @pl.when(band == 1)
        def _():
            img[x] = img[x] + times(theirs(x), coef[1]).reshape(NJ, CY, 128)

        return carry

    bounds = (0, 2, 7, 12, 12)
    for n in range(4):
        copies = send(1, n)
        lax.fori_loop(bounds[n], bounds[n + 1], turn, 0)
        if n == 3:
            stores = [
                pltpu.make_async_copy(
                    img.at[:, j], out_ref.at[0, 0, :, :, pl.ds(128 * j, 128)], load_sem.at[j]
                )
                for j in range(NJ)
            ]
            for copy in stores:
                copy.start()
        collect(1, n, copies)

    matrix(1, work.at[1])
    pick = (
        lax.broadcasted_iota(jnp.int32, (128, n_orb), 0)
        == n_orb + lax.broadcasted_iota(jnp.int32, (128, n_orb), 1)
    ).astype(jnp.float32)
    inv = jnp.dot(work[0], pick, precision=HIGHEST, preferred_element_type=jnp.float32)
    left = jnp.dot(
        inv, work[1, :, 0:n_orb], precision=HIGHEST, preferred_element_type=jnp.float32
    )
    proj_ref[...] = lax.dot_general(
        left,
        inv,
        (((1,), (1,)), ((), ())),
        precision=HIGHEST,
        preferred_element_type=jnp.float32,
    )
    for copy in stores:
        copy.wait()
    drain(first)
    drain(second)
    drain(third)

    @pl.when(band == 0)
    def _():
        rest.wait_send()

    @pl.when(band == 1)
    def _():
        lower.wait_send()


def local(orbitals, potential):
    big = (XO * 2 + CX, JO * 2 + NJ, YO * 2 + CY, 128)
    tile = (CX, NJ, CY, 128)
    vmem = pl.BlockSpec(memory_space=pltpu.VMEM)
    hbm = pl.BlockSpec(memory_space=pl.ANY)
    f32 = jnp.float32
    dma = pltpu.SemaphoreType.DMA
    return pl.pallas_call(
        filter_kernel,
        out_shape=(
            jax.ShapeDtypeStruct((1, 1, CX, CY, CZ * OB), f32),
            jax.ShapeDtypeStruct((2 * OB, 2 * OB), f32),
        ),
        in_specs=[hbm, vmem],
        out_specs=(hbm, vmem),
        scratch_shapes=[
            pltpu.VMEM(big, f32),
            pltpu.VMEM(big, f32),
            pltpu.VMEM(big, f32),
            pltpu.VMEM(tile, f32),
            pltpu.VMEM(tile, f32),
            pltpu.VMEM(tile, f32),
            pltpu.VMEM((2, 4, 2, OB // 2, 128), f32),
            pltpu.VMEM((2, 24, OB // 2, 128), f32),
            pltpu.VMEM((2, 2 * OB, 128), f32),
            pltpu.VMEM((2, 128, 128), f32),
            dma((NJ,)),
            dma((3, 6)),
            dma((3, 6)),
            dma((3,)),
            dma((3,)),
            dma((2, 24)),
            dma((2, 24)),
        ],
        compiler_params=pltpu.CompilerParams(
            collective_id=0, has_side_effects=True, vmem_limit_bytes=48 << 20
        ),
    )(orbitals, potential)


def solution(mesh):
    return jax.shard_map(
        local,
        mesh=mesh,
        in_specs=(P("dom", "band", None, None, None), P("dom", None, None, None)),
        out_specs=(P("dom", "band", None, None, None), P()),
        check_vma=False,
    )
```

time: 248 us -> 213 us (0.86)
  Pallas kernels: 226 us -> 207 us
  other arithmetic: 13.1 us -> 0 us
    pallas_call x2 -> x1, Pallas kernels: 226 us -> 207 us  [local(): pl.pallas_call(filter_kernel, out_shape=(jax.ShapeDtypeStruct((1, 1, CX,...]
    another operation x6 -> x0, other arithmetic: 12.7 us -> none  [the longest x3 6.53 us: local(): lower = jnp.linalg.cholesky(corr)]
where the time goes in v2:
time: 213 us; the launch traced here: 212 us
  Pallas kernels  207 us (97%)
  local copies, waits for them, and re-layouts  4.09 us (2%)
    pallas_call x1, Pallas kernels, local(): pl.pallas_call(filter_kernel, out_shape=(jax.ShapeDtypeStruct((1, 1, CX,...  207 us

profile of v2, /device:TPU:33, one launch (start us, length us, event | category | flops | bytes accessed | tf_op | source)
XLA Modules:
  0.0 211.7 jit_solution(6174333803566346025)
XLA Ops:
  0.6 0.0 copy-start
  0.6 1.4 copy-done
  2.0 0.0 copy-start.1
  2.0 0.9 copy-done.1
  3.0 207.0 %shard_map.41 = (f32[1,1,12,32,1024]{4,3,2,1,0:T(8,128)S(1)}, f32[64,64]{1,0:T(8,128)S(1)}) custom-call(f32[1,1,12,32,1024]{4,3,2,1,0:T(8,128)S(1)} %copy-done, f32[1,12,32,32]{3,2,1,0:T(8,128)S(1)} %copy-done.1), custom_call_target="tpu_custom_call" | custom-call | tf_op jit(solution)/shard_map/pallas_call | solution.py:505
  209.9 1.1 copy.6
  211.1 0.6 copy.7
Async XLA Ops:
  0.6 1.4 copy-start
  2.0 0.9 copy-start.1

commit v3 on v2

--- a/solution.py
+++ b/solution.py
@@ -67,9 +67,41 @@
     return out
 
 
+def forward_stencil(field, pot, x):
+    lane = lax.broadcasted_iota(jnp.int32, (CY, 128), 1)
+
+    def tile(j, dx=0, dy=0):
+        return field[XO + x + dx, JO + j, pl.ds(YO + dy, CY), :]
+
+    def partial(j):
+        v, p1 = tile(j), tile(j + 1)
+        return (
+            pltpu.roll(A[1] * v + A[5] * p1, 96, 1),
+            pltpu.roll(A[2] * v + A[6] * p1, 64, 1),
+            pltpu.roll(A[3] * v, 32, 1),
+        )
+
+    out = []
+    low = partial(0)
+    for j in range(NJ):
+        high = partial(j + 1)
+        acc = jnp.where(lane < 96, low[0], high[0])
+        acc = acc + jnp.where(lane < 64, low[1], high[1])
+        acc = acc + jnp.where(lane < 32, low[2], high[2])
+        low = high
+        acc = acc + 0.5 * pot[x, j] * tile(j)
+        for k in range(1, 7):
+            terms = tile(j, k) + tile(j, 0, k)
+            if k == 4:
+                terms = terms + tile(j + 1)
+            acc = acc + A[k] * terms
+        out.append(acc)
+    return out
+
+
 def filter_kernel(
     orb_ref,
-    pot_ref,
+    pot_hbm,
     out_ref,
     proj_ref,
     e0,
@@ -82,7 +114,9 @@
     recv,
     work,
     coef,
+    pot_ref,
     load_sem,
+    out_sem,
     hs,
     hr,
     bs,
@@ -105,6 +139,7 @@
         )
         for j in range(NJ)
     ]
+    loads.append(pltpu.make_async_copy(pot_hbm, pot_ref, load_sem.at[NJ]))
     for copy in loads:
         copy.start()
 
@@ -253,11 +288,12 @@
         return carry
 
     lax.fori_loop(0, CX, step_two, 0)
-    low, high = pl.ds(0, CX // 2), pl.ds(CX // 2, CX // 2)
+    third = halo(e2, 2)[1::2]
+    start(third, e2)
     partner = (dom, 1 - band)
-
-    def across(planes, at):
-        return pltpu.make_async_remote_copy(
+    parts = (pl.ds(0, CX // 2), pl.ds(CX // 2, CX // 2))
+    across = [
+        pltpu.make_async_remote_copy(
             e2.at[pl.ds(XO + planes.start, planes.size), OWN[1], OWN[2]],
             other.at[planes],
             bs.at[at],
@@ -265,19 +301,10 @@
             device_id=partner,
             device_id_type=MESH,
         )
-
-    upper, lower, rest = across(high, 0), across(low, 1), across(low, 2)
-
-    @pl.when(band == 0)
-    def _():
-        upper.start()
-
-    @pl.when(band == 1)
-    def _():
-        lower.start()
-
-    third = halo(e2, 2)
-    start(third, e2)
+        for at, planes in enumerate(parts)
+    ]
+    for copy in across:
+        copy.start()
 
     def own(x):
         return e2[XO + x, pl.ds(JO, NJ), pl.ds(YO, CY), :].reshape(NJ * CY, 128)
@@ -288,7 +315,7 @@
     def image(x):
         return img[x].reshape(NJ * CY, 128)
 
-    def gram(left, right, begin, end):
+    def gram(left, right, begin, end, wide):
         def add(x, acc):
             return acc + lax.dot_general(
                 left(x),
@@ -298,93 +325,112 @@
                 preferred_element_type=jnp.float32,
             )
 
-        acc = lax.fori_loop(begin, end, add, jnp.zeros((128, 128), jnp.float32))
-        total = acc[:OB, :OB]
+        return lax.fori_loop(begin, end, add, jnp.zeros((128, wide), jnp.float32))
+
+    def block(acc, at):
+        total = acc[:OB, at : at + OB]
         for g in range(1, 4):
-            total = total + acc[OB * g : OB * (g + 1), OB * g : OB * (g + 1)]
+            total = total + acc[OB * g : OB * (g + 1), at + OB * g : at + OB * (g + 1)]
         return total
 
-    def stage_copies(which, n):
-        source = part.at[which, 0, 1 - core] if n == 0 else part.at[which, n, 0]
-        return [
+    def both(x):
+        return jnp.concatenate([own(x), image(x)], axis=1)
+
+    def add_up(n):
+        source = part.at[0, 1 - core] if n == 0 else part.at[n, 0]
+        copies = [
             pltpu.make_async_remote_copy(
                 source,
-                recv.at[which, slots[n] + k],
-                rs.at[which, slots[n] + k],
-                rr.at[which, slots[n] + k],
+                recv.at[slots[n] + k],
+                rs.at[slots[n] + k],
+                rr.at[slots[n] + k],
                 device_id=peer,
                 device_id_type=MESH,
             )
             for k, peer in enumerate(stages[n])
         ]
-
-    def send(which, n):
-        copies = stage_copies(which, n)
         for copy in copies:
             copy.start()
-        return copies
-
-    def collect(which, n, copies):
         for copy in copies:
             copy.wait()
-        total = part[which, 0, core] if n == 0 else part[which, n, 0]
+        total = part[0, core] if n == 0 else part[n, 0]
         if n == 3:
-            part[which, 0, core] = total
-            part[which, 0, 1 - core] = recv[which, slots[3]]
+            part[0, core] = total
+            part[0, 1 - core] = recv[slots[3]]
             return
         for k in range(len(copies)):
-            total = total + recv[which, slots[n] + k]
-        part[which, n + 1, 0] = total
-
-    def put(which, column, block):
+            total = total + recv[slots[n] + k]
+        part[n + 1, 0] = total
+
+    def put(which, column, value):
         for half in range(2):
-            part[which, 0, half, :, OB * column : OB * (column + 1)] = block[
+            part[0, half, which, :, OB * column : OB * (column + 1)] = value[
                 half * (OB // 2) : (half + 1) * (OB // 2)
             ]
 
     part[...] = jnp.zeros_like(part)
-    mine = gram(own, own, 0, CX)
+    arrive(third)
+
+    def step_three(x, carry):
+        for j, value in enumerate(forward_stencil(e2, pot, x)):
+            img[x, j] = value
+        return carry
+
+    lax.fori_loop(0, CX, step_three, 0)
+    mine = gram(own, both, 0, CX, 256)
 
     @pl.when(band == 0)
     def _():
-        put(0, 0, mine)
-        upper.wait_send()
-        rest.start()
-        lower.wait_recv()
-        put(0, 1, gram(own, theirs, 0, CX // 2))
+        put(0, 0, block(mine, 0))
+        put(1, 0, block(mine, 128))
+        across[0].wait_recv()
+        crossed = gram(theirs, image, 0, CX // 2, 128)
+        across[1].wait_recv()
+        crossed = crossed + gram(theirs, image, CX // 2, CX, 128)
+        put(1, 2, block(crossed, 0))
 
     @pl.when(band == 1)
     def _():
-        put(0, 2, mine)
-        upper.wait_recv()
-        put(0, 1, gram(theirs, own, CX // 2, CX))
+        put(0, 2, block(mine, 0))
+        put(1, 3, block(mine, 128))
+        across[0].wait_recv()
+        crossed = gram(theirs, both, 0, CX // 2, 256)
+        across[1].wait_recv()
+        crossed = crossed + gram(theirs, both, CX // 2, CX, 256)
+        put(0, 1, block(crossed, 0))
+        put(1, 1, block(crossed, 128))
 
     for n in range(4):
-        collect(0, n, send(0, n))
+        add_up(n)
 
     eye = (
         lax.broadcasted_iota(jnp.int32, (OB, OB), 0) == lax.broadcasted_iota(jnp.int32, (OB, OB), 1)
     ).astype(jnp.float32)
 
-    def matrix(which, dst):
-        blocks = part[which, 0].reshape(OB, 128) * (1.0 / CELLS)
-        cross = blocks[:, OB : 2 * OB]
-        dst[0:OB, 0:OB] = blocks[:, 0:OB]
-        dst[0:OB, OB : 2 * OB] = cross
-        dst[OB : 2 * OB, OB : 2 * OB] = blocks[:, 2 * OB : 3 * OB]
-        dst[OB : 2 * OB, 0:OB] = lax.dot_general(
-            cross,
+    def flip(m):
+        return lax.dot_general(
+            m,
             eye,
             (((0,), (0,)), ((), ())),
             precision=HIGHEST,
             preferred_element_type=jnp.float32,
         )
 
+    def sums(which):
+        rows = jnp.concatenate([part[0, 0, which], part[0, 1, which]], axis=0) * (1.0 / CELLS)
+        return [rows[:, OB * k : OB * (k + 1)] for k in range(4)]
+
+    def matrix(dst, a00, a01, a11):
+        dst[0:OB, 0:OB] = a00
+        dst[0:OB, OB : 2 * OB] = a01
+        dst[OB : 2 * OB, OB : 2 * OB] = a11
+        dst[OB : 2 * OB, 0:OB] = flip(a01)
+
     n_orb = 2 * OB
     row_id = lax.broadcasted_iota(jnp.int32, (n_orb, 128), 0)
     lane_id = lax.broadcasted_iota(jnp.int32, (n_orb, 128), 1)
     work[0] = (lane_id == row_id + n_orb).astype(jnp.float32)
-    matrix(0, work.at[0])
+    matrix(work.at[0], *sums(0)[:3])
 
     def eliminate(k, m):
         pivot_row = jnp.sum(jnp.where(row_id == k, m, 0.0), axis=0, keepdims=True)
@@ -410,26 +456,6 @@
 
     coef[0] = weights(band)
     coef[1] = weights(0)
-
-    arrive(third)
-
-    def step_three(x, carry):
-        for j, value in enumerate(stencil(e2, pot, x)):
-            img[x, j] = value
-        return carry
-
-    lax.fori_loop(0, CX, step_three, 0)
-    ham = gram(own, image, 0, CX)
-
-    @pl.when(band == 0)
-    def _():
-        put(1, 0, ham)
-
-    @pl.when(band == 1)
-    def _():
-        put(1, 2, ham)
-        rest.wait_recv()
-        put(1, 1, gram(theirs, image, 0, CX))
 
     def turn(x, carry):
         def times(rows, w):
@@ -449,22 +475,21 @@
 
         return carry
 
-    bounds = (0, 2, 7, 12, 12)
-    for n in range(4):
-        copies = send(1, n)
-        lax.fori_loop(bounds[n], bounds[n + 1], turn, 0)
-        if n == 3:
-            stores = [
+    stores = []
+    for half in range(2):
+        lax.fori_loop(half * CX // 2, (half + 1) * CX // 2, turn, 0)
+        for j in range(NJ):
+            stores.append(
                 pltpu.make_async_copy(
-                    img.at[:, j], out_ref.at[0, 0, :, :, pl.ds(128 * j, 128)], load_sem.at[j]
+                    img.at[parts[half], j],
+                    out_ref.at[0, 0, parts[half], :, pl.ds(128 * j, 128)],
+                    out_sem.at[half, j],
                 )
-                for j in range(NJ)
-            ]
-            for copy in stores:
-                copy.start()
-        collect(1, n, copies)
-
-    matrix(1, work.at[1])
+            )
+            stores[-1].start()
+
+    s00, s01, s10, s11 = sums(1)
+    matrix(work.at[1], s00 + flip(s00), s01 + flip(s10), s11 + flip(s11))
     pick = (
         lax.broadcasted_iota(jnp.int32, (128, n_orb), 0)
         == n_orb + lax.broadcasted_iota(jnp.int32, (128, n_orb), 1)
@@ -485,14 +510,8 @@
     drain(first)
     drain(second)
     drain(third)
-
-    @pl.when(band == 0)
-    def _():
-        rest.wait_send()
-
-    @pl.when(band == 1)
-    def _():
-        lower.wait_send()
+    for copy in across:
+        copy.wait_send()
 
 
 def local(orbitals, potential):
@@ -508,7 +527,7 @@
             jax.ShapeDtypeStruct((1, 1, CX, CY, CZ * OB), f32),
             jax.ShapeDtypeStruct((2 * OB, 2 * OB), f32),
         ),
-        in_specs=[hbm, vmem],
+        in_specs=[hbm, hbm],
         out_specs=(hbm, vmem),
         scratch_shapes=[
             pltpu.VMEM(big, f32),
@@ -517,20 +536,22 @@
             pltpu.VMEM(tile, f32),
             pltpu.VMEM(tile, f32),
             pltpu.VMEM(tile, f32),
-            pltpu.VMEM((2, 4, 2, OB // 2, 128), f32),
-            pltpu.VMEM((2, 24, OB // 2, 128), f32),
+            pltpu.VMEM((4, 2, 2, OB // 2, 128), f32),
+            pltpu.VMEM((24, 2, OB // 2, 128), f32),
             pltpu.VMEM((2, 2 * OB, 128), f32),
             pltpu.VMEM((2, 128, 128), f32),
-            dma((NJ,)),
+            pltpu.VMEM((1, CX, CY, CZ), f32),
+            dma((NJ + 1,)),
+            dma((2, NJ)),
             dma((3, 6)),
             dma((3, 6)),
-            dma((3,)),
-            dma((3,)),
-            dma((2, 24)),
-            dma((2, 24)),
+            dma((2,)),
+            dma((2,)),
+            dma((24,)),
+            dma((24,)),
         ],
         compiler_params=pltpu.CompilerParams(
-            collective_id=0, has_side_effects=True, vmem_limit_bytes=48 << 20
+            collective_id=0, has_side_effects=True, vmem_limit_bytes=60 << 20
         ),
     )(orbitals, potential)
 

time: 213 us -> 206 us (0.967)
  Pallas kernels: 207 us -> 202 us
    pallas_call x1, Pallas kernels: 207 us -> 202 us  [local(): pl.pallas_call(filter_kernel, out_shape=(jax.ShapeDtypeStruct((1, 1, CX,...]
where the time goes in v3:
time: 206 us
  Pallas kernels  202 us (98%)
  local copies, waits for them, and re-layouts  3.35 us (2%)
    pallas_call x1, Pallas kernels, local(): pl.pallas_call(filter_kernel, out_shape=(jax.ShapeDtypeStruct((1, 1, CX,...  202 us

profile of v3, /device:TPU:33, one launch (start us, length us, event | category | flops | bytes accessed | tf_op | source)
XLA Modules:
  0.0 205.9 jit_solution(17906554966698449969)
XLA Ops:
  0.6 201.9 %shard_map.41 = (f32[1,1,12,32,1024]{4,3,2,1,0:T(8,128)}, f32[64,64]{1,0:T(8,128)}) custom-call(f32[1,1,12,32,1024]{4,3,2,1,0:T(8,128)} %orb_ref.1, f32[1,12,32,32]{3,2,1,0:T(8,128)} %pot_hbm.1), custom_call_target="tpu_custom_call" | custom-call | tf_op jit(solution)/shard_map/pallas_call | solution.py:524
  202.6 0.0 copy-start
  202.6 2.7 %copy.6 = f32[1,1,12,32,1024]{4,3,2,1,0:T(8,128)} copy(f32[1,1,12,32,1024]{4,3,2,1,0:T(8,128)} %get-tuple-element.4) | data formatting | bytes 3145728
  205.3 0.0 copy-done
  205.3 0.6 copy.7
Async XLA Ops:
  202.6 2.7 %copy-start = (f32[64,64]{1,0:T(8,128)S(1)}, f32[64,64]{1,0:T(8,128)}, u32[]{:S(2)}) copy-start(f32[64,64]{1,0:T(8,128)} %get-tuple-element.5) | copy-start | bytes 49156

commit v4 on v3

--- a/solution.py
+++ b/solution.py
@@ -67,18 +67,18 @@
     return out
 
 
-def forward_stencil(field, pot, x):
+def backward_stencil(field, pot, x):
     lane = lax.broadcasted_iota(jnp.int32, (CY, 128), 1)
 
     def tile(j, dx=0, dy=0):
         return field[XO + x + dx, JO + j, pl.ds(YO + dy, CY), :]
 
     def partial(j):
-        v, p1 = tile(j), tile(j + 1)
+        m1, m2 = tile(j - 1), tile(j - 2)
         return (
-            pltpu.roll(A[1] * v + A[5] * p1, 96, 1),
-            pltpu.roll(A[2] * v + A[6] * p1, 64, 1),
-            pltpu.roll(A[3] * v, 32, 1),
+            pltpu.roll(A[3] * m1, 96, 1),
+            pltpu.roll(A[2] * m1 + A[6] * m2, 64, 1),
+            pltpu.roll(A[1] * m1 + A[5] * m2, 32, 1),
         )
 
     out = []
@@ -91,9 +91,9 @@
         low = high
         acc = acc + 0.5 * pot[x, j] * tile(j)
         for k in range(1, 7):
-            terms = tile(j, k) + tile(j, 0, k)
+            terms = tile(j, -k) + tile(j, 0, -k)
             if k == 4:
-                terms = terms + tile(j + 1)
+                terms = terms + tile(j - 1)
             acc = acc + A[k] * terms
         out.append(acc)
     return out
@@ -111,6 +111,10 @@
     pot,
     other,
     part,
+    gathered,
+    halved,
+    piece,
+    summed,
     recv,
     work,
     coef,
@@ -164,8 +168,6 @@
         for k in range(4)
         if i or k
     ]
-    stages = ((twin,), column, plane, (twin,))
-    slots = (0, 1, 8, 23)
 
     barrier = pltpu.get_barrier_semaphore()
     count = jnp.int32(23)
@@ -288,7 +290,7 @@
         return carry
 
     lax.fori_loop(0, CX, step_two, 0)
-    third = halo(e2, 2)[1::2]
+    third = halo(e2, 2)[0::2]
     start(third, e2)
     partner = (dom, 1 - band)
     parts = (pl.ds(0, CX // 2), pl.ds(CX // 2, CX // 2))
@@ -336,43 +338,58 @@
     def both(x):
         return jnp.concatenate([own(x), image(x)], axis=1)
 
-    def add_up(n):
-        source = part.at[0, 1 - core] if n == 0 else part.at[n, 0]
-        copies = [
-            pltpu.make_async_remote_copy(
-                source,
-                recv.at[slots[n] + k],
-                rs.at[slots[n] + k],
-                rr.at[slots[n] + k],
-                device_id=peer,
-                device_id_type=MESH,
-            )
-            for k, peer in enumerate(stages[n])
-        ]
+    def swap(copies):
         for copy in copies:
             copy.start()
         for copy in copies:
             copy.wait()
-        total = part[0, core] if n == 0 else part[n, 0]
-        if n == 3:
-            part[0, core] = total
-            part[0, 1 - core] = recv[slots[3]]
-            return
-        for k in range(len(copies)):
-            total = total + recv[slots[n] + k]
-        part[n + 1, 0] = total
+
+    def message(source, dest, slot, peer):
+        return pltpu.make_async_remote_copy(
+            source, dest, rs.at[slot], rr.at[slot], device_id=peer, device_id_type=MESH
+        )
+
+    def add_up():
+        swap([message(part.at[1 - core], gathered, 0, twin)])
+        halved[...] = part[core] + gathered[...]
+        swap(
+            [
+                message(halved.at[lax.rem(pz + (k + 1) // 2, 4)], recv.at[k], 1 + k, peer)
+                for k, peer in enumerate(column)
+            ]
+        )
+        total = halved[pz]
+        for k in range(len(column)):
+            total = total + recv[k]
+        piece[0] = total
+        swap(
+            [
+                message(piece.at[0], recv.at[7 + k], 8 + k, peer)
+                for k, peer in enumerate(plane)
+            ]
+        )
+        for k in range(len(plane)):
+            total = total + recv[7 + k]
+        summed[core, pz] = total
+        swap(
+            [
+                message(summed.at[core, pz], summed.at[core, pz], 22 + k, column[2 * k - 1])
+                for k in range(1, 4)
+            ]
+        )
+        swap([message(summed.at[core], summed.at[core], 26, twin)])
 
     def put(which, column, value):
         for half in range(2):
-            part[0, half, which, :, OB * column : OB * (column + 1)] = value[
-                half * (OB // 2) : (half + 1) * (OB // 2)
-            ]
+            for t in range(2):
+                at = half * (OB // 2) + 8 * t
+                part[half, 2 * which + t, :, OB * column : OB * (column + 1)] = value[at : at + 8]
 
     part[...] = jnp.zeros_like(part)
     arrive(third)
 
     def step_three(x, carry):
-        for j, value in enumerate(forward_stencil(e2, pot, x)):
+        for j, value in enumerate(backward_stencil(e2, pot, x)):
             img[x, j] = value
         return carry
 
@@ -400,8 +417,7 @@
         put(0, 1, block(crossed, 0))
         put(1, 1, block(crossed, 128))
 
-    for n in range(4):
-        add_up(n)
+    add_up()
 
     eye = (
         lax.broadcasted_iota(jnp.int32, (OB, OB), 0) == lax.broadcasted_iota(jnp.int32, (OB, OB), 1)
@@ -417,7 +433,8 @@
         )
 
     def sums(which):
-        rows = jnp.concatenate([part[0, 0, which], part[0, 1, which]], axis=0) * (1.0 / CELLS)
+        pieces = [summed[half, 2 * which + t] for half in range(2) for t in range(2)]
+        rows = jnp.concatenate(pieces, axis=0) * (1.0 / CELLS)
         return [rows[:, OB * k : OB * (k + 1)] for k in range(4)]
 
     def matrix(dst, a00, a01, a11):
@@ -432,14 +449,27 @@
     work[0] = (lane_id == row_id + n_orb).astype(jnp.float32)
     matrix(work.at[0], *sums(0)[:3])
 
-    def eliminate(k, m):
-        pivot_row = jnp.sum(jnp.where(row_id == k, m, 0.0), axis=0, keepdims=True)
-        pivot_col = jnp.sum(jnp.where(lane_id == k, m, 0.0), axis=1, keepdims=True)
-        pivot = jnp.sum(jnp.where(lane_id[:1] == k, pivot_row, 0.0), axis=1, keepdims=True)
-        factor = jnp.where(row_id > k, pivot_col * (1.0 / pivot), 0.0)
-        return m - factor * pivot_row
-
-    m = lax.fori_loop(0, n_orb, eliminate, work[0])
+    def eliminate(step, m):
+        k = 2 * step
+        row0 = jnp.sum(jnp.where(row_id == k, m, 0.0), axis=0, keepdims=True)
+        row1 = jnp.sum(jnp.where(row_id == k + 1, m, 0.0), axis=0, keepdims=True)
+        col0 = jnp.sum(jnp.where(lane_id == k, m, 0.0), axis=1, keepdims=True)
+        col1 = jnp.sum(jnp.where(lane_id == k + 1, m, 0.0), axis=1, keepdims=True)
+
+        def entry(row, at):
+            return jnp.sum(jnp.where(lane_id[:1] == at, row, 0.0), axis=1, keepdims=True)
+
+        inv0 = 1.0 / entry(row0, k)
+        ratio0 = entry(row1, k) * inv0
+        across0 = entry(row0, k + 1)
+        row1 = row1 - ratio0 * row0
+        pivot1 = entry(row1, k + 1)
+        col1 = col1 - (across0 * inv0) * col0
+        factor0 = jnp.where(row_id > k, col0 * inv0, 0.0)
+        factor1 = jnp.where(row_id > k + 1, col1 * (1.0 / pivot1), 0.0)
+        return m - factor0 * row0 - factor1 * row1
+
+    m = lax.fori_loop(0, n_orb // 2, eliminate, work[0])
     diag = jnp.sum(jnp.where(lane_id == row_id, m, 0.0), axis=1, keepdims=True)
     inverse = m * (1.0 / jnp.sqrt(diag))
     work[0] = inverse
@@ -536,8 +566,12 @@
             pltpu.VMEM(tile, f32),
             pltpu.VMEM(tile, f32),
             pltpu.VMEM(tile, f32),
-            pltpu.VMEM((4, 2, 2, OB // 2, 128), f32),
-            pltpu.VMEM((24, 2, OB // 2, 128), f32),
+            pltpu.VMEM((2, 4, 8, 128), f32),
+            pltpu.VMEM((4, 8, 128), f32),
+            pltpu.VMEM((4, 8, 128), f32),
+            pltpu.VMEM((1, 8, 128), f32),
+            pltpu.VMEM((2, 4, 8, 128), f32),
+            pltpu.VMEM((22, 8, 128), f32),
             pltpu.VMEM((2, 2 * OB, 128), f32),
             pltpu.VMEM((2, 128, 128), f32),
             pltpu.VMEM((1, CX, CY, CZ), f32),
@@ -547,8 +581,8 @@
             dma((3, 6)),
             dma((2,)),
             dma((2,)),
-            dma((24,)),
-            dma((24,)),
+            dma((27,)),
+            dma((27,)),
         ],
         compiler_params=pltpu.CompilerParams(
             collective_id=0, has_side_effects=True, vmem_limit_bytes=60 << 20

time: 206 us -> 192 us (0.932)
  Pallas kernels: 202 us -> 188 us
    pallas_call x1, Pallas kernels: 202 us -> 188 us  [local(): pl.pallas_call(filter_kernel, out_shape=(jax.ShapeDtypeStruct((1, 1, CX,...]
where the time goes in v4:
time: 192 us
  Pallas kernels  188 us (98%)
  local copies, waits for them, and re-layouts  3.35 us (2%)
    pallas_call x1, Pallas kernels, local(): pl.pallas_call(filter_kernel, out_shape=(jax.ShapeDtypeStruct((1, 1, CX,...  188 us

profile of v4, /device:TPU:33, one launch (start us, length us, event | category | flops | bytes accessed | tf_op | source)
XLA Modules:
  0.0 191.9 jit_solution(6197960851307602308)
XLA Ops:
  0.6 187.9 %shard_map.41 = (f32[1,1,12,32,1024]{4,3,2,1,0:T(8,128)}, f32[64,64]{1,0:T(8,128)}) custom-call(f32[1,1,12,32,1024]{4,3,2,1,0:T(8,128)} %orb_ref.1, f32[1,12,32,32]{3,2,1,0:T(8,128)} %pot_hbm.1), custom_call_target="tpu_custom_call" | custom-call | tf_op jit(solution)/shard_map/pallas_call | solution.py:554
  188.5 0.0 copy-start
  188.5 2.7 %copy.6 = f32[1,1,12,32,1024]{4,3,2,1,0:T(8,128)} copy(f32[1,1,12,32,1024]{4,3,2,1,0:T(8,128)} %get-tuple-element.4) | data formatting | bytes 3145728
  191.3 0.0 copy-done
  191.3 0.6 copy.7
Async XLA Ops:
  188.5 2.7 %copy-start = (f32[64,64]{1,0:T(8,128)S(1)}, f32[64,64]{1,0:T(8,128)}, u32[]{:S(2)}) copy-start(f32[64,64]{1,0:T(8,128)} %get-tuple-element.5) | copy-start | bytes 49156

commit v5 on v4

--- a/solution.py
+++ b/solution.py
@@ -231,7 +231,7 @@
             )
             copies.append((up, at < n - 1, at > 0, below))
             copies.append((down, at > 0, at < n - 1, above))
-        return copies
+        return [copies[i] for i in (4, 5, 2, 3, 0, 1)]
 
     def start(copies, field):
         for copy, sends, receives, landing in copies:

time: 192 us -> 191 us (level)
  no operation moved by 1% of the time
where the time goes in v5:
time: 191 us
  Pallas kernels  187 us (98%)
  local copies, waits for them, and re-layouts  3.35 us (2%)
    pallas_call x1, Pallas kernels, local(): pl.pallas_call(filter_kernel, out_shape=(jax.ShapeDtypeStruct((1, 1, CX,...  187 us

profile of v5, /device:TPU:33, one launch (start us, length us, event | category | flops | bytes accessed | tf_op | source)
XLA Modules:
  0.0 191.0 jit_solution(17456034215393247726)
XLA Ops:
  0.6 187.0 %shard_map.41 = (f32[1,1,12,32,1024]{4,3,2,1,0:T(8,128)}, f32[64,64]{1,0:T(8,128)}) custom-call(f32[1,1,12,32,1024]{4,3,2,1,0:T(8,128)} %orb_ref.1, f32[1,12,32,32]{3,2,1,0:T(8,128)} %pot_hbm.1), custom_call_target="tpu_custom_call" | custom-call | tf_op jit(solution)/shard_map/pallas_call | solution.py:554
  187.6 0.0 copy-start
  187.6 2.7 %copy.6 = f32[1,1,12,32,1024]{4,3,2,1,0:T(8,128)} copy(f32[1,1,12,32,1024]{4,3,2,1,0:T(8,128)} %get-tuple-element.4) | data formatting | bytes 3145728
  190.4 0.0 copy-done
  190.4 0.6 copy.7
Async XLA Ops:
  187.6 2.7 %copy-start = (f32[64,64]{1,0:T(8,128)S(1)}, f32[64,64]{1,0:T(8,128)}, u32[]{:S(2)}) copy-start(f32[64,64]{1,0:T(8,128)} %get-tuple-element.5) | copy-start | bytes 49156

commit v6 on v5

--- a/solution.py
+++ b/solution.py
@@ -469,7 +469,7 @@
         factor1 = jnp.where(row_id > k + 1, col1 * (1.0 / pivot1), 0.0)
         return m - factor0 * row0 - factor1 * row1
 
-    m = lax.fori_loop(0, n_orb // 2, eliminate, work[0])
+    m = lax.fori_loop(0, n_orb // 2, eliminate, work[0], unroll=4)
     diag = jnp.sum(jnp.where(lane_id == row_id, m, 0.0), axis=1, keepdims=True)
     inverse = m * (1.0 / jnp.sqrt(diag))
     work[0] = inverse

time: 191 us -> 191 us (level)
  no operation moved by 1% of the time
where the time goes in v6:
time: 191 us
  Pallas kernels  187 us (98%)
  local copies, waits for them, and re-layouts  3.35 us (2%)
    pallas_call x1, Pallas kernels, local(): pl.pallas_call(filter_kernel, out_shape=(jax.ShapeDtypeStruct((1, 1, CX,...  187 us

profile of v6, /device:TPU:33, one launch (start us, length us, event | category | flops | bytes accessed | tf_op | source)
XLA Modules:
  0.0 190.9 jit_solution(14731893293186398558)
XLA Ops:
  0.6 186.9 %shard_map.41 = (f32[1,1,12,32,1024]{4,3,2,1,0:T(8,128)}, f32[64,64]{1,0:T(8,128)}) custom-call(f32[1,1,12,32,1024]{4,3,2,1,0:T(8,128)} %orb_ref.1, f32[1,12,32,32]{3,2,1,0:T(8,128)} %pot_hbm.1), custom_call_target="tpu_custom_call" | custom-call | tf_op jit(solution)/shard_map/pallas_call | solution.py:554
  187.5 0.0 copy-start
  187.5 2.7 %copy.6 = f32[1,1,12,32,1024]{4,3,2,1,0:T(8,128)} copy(f32[1,1,12,32,1024]{4,3,2,1,0:T(8,128)} %get-tuple-element.4) | data formatting | bytes 3145728
  190.2 0.0 copy-done
  190.3 0.6 copy.7
Async XLA Ops:
  187.5 2.7 %copy-start = (f32[64,64]{1,0:T(8,128)S(1)}, f32[64,64]{1,0:T(8,128)}, u32[]{:S(2)}) copy-start(f32[64,64]{1,0:T(8,128)} %get-tuple-element.5) | copy-start | bytes 49156
